TPU v7x, 128 devices: a whole 4x4x4 slice. The times are simulated.
128 devices in a mesh: tm: 8 (over y, core), tensor: 16 (over z, x).
Axes of the slice: x: 4, y: 4, z: 4, core: 2. Of those that a mesh axis runs over, the one named last changes fastest.
Arguments:
- queries: bfloat16 [5120, 4096], P('tm', 'tensor'), may hold values from -6 to 6
- keys: bfloat16 [5120, 4096], P('tm', 'tensor'), may hold values from -6 to 6
- values: bfloat16 [5120, 4096], P('tm', 'tensor'), may hold values from -6 to 6
- grad_out: bfloat16 [5120, 5120], P('tm', 'tensor'), may hold values from -18 to 18
- frame_map: int32 [8], replicated, may hold values from 0 to 7, as said below
- band: int32 [8, 8], replicated, may hold values from -1 to 640, as said below
- w_query: bfloat16 [5120, 4096], P(None, 'tensor'), may hold values from -0.75 to 0.75
- w_key: bfloat16 [5120, 4096], P(None, 'tensor'), may hold values from -0.75 to 0.75
- w_value: bfloat16 [5120, 4096], P(None, 'tensor'), may hold values from -0.75 to 0.75
- w_out: bfloat16 [4096, 5120], P('tensor'), may hold values from -0.09375 to 0.09375
Outputs:
- input_grad: bfloat16 [5120, 5120], P('tensor', 'tm')
Inputs may be any that keep to these rules, and one draw needn't show every extreme that they name: `frame_map`: each latent frame is held by exactly one slot. band[i][j] is 640 where i == j, -1 (nothing attends) where |i - j| > 4, and otherwise between half of and all of 640 // 2**ceil(log2 |i - j|), rounded down.
All inputs are finite; a program needn't handle non-finite values.
Results may differ from a plain program's by a relative error of at most 0.023.
Values may be sent and summed in bfloat16 or wider, within the bound.
A program may use at most 192 MiB of HBM per device.

v0:
```python
import jax
import jax.numpy as jnp
from jax import lax
from jax.sharding import PartitionSpec as P

HD = 128


masked_score = -1e30


def run_block(update, totals):
    result = update(totals)
    return result


def block_grads(
    query_piece, grad_piece, key_piece, value_piece, log_piece, dot_piece, allowed, score_scale
):
    scores = (
        jnp.einsum("qhd,khd->hqk", query_piece, key_piece, preferred_element_type=jnp.float32)
        * score_scale
    )
    probs = jnp.where(allowed, jnp.exp(scores - log_piece[..., None]), 0.0)
    grad_probs = jnp.einsum(
        "qhd,khd->hqk", grad_piece, value_piece, preferred_element_type=jnp.float32
    )
    grad_scores = (probs * (grad_probs - dot_piece[..., None])).astype(jnp.bfloat16)
    return (probs.astype(jnp.bfloat16), grad_scores)


def per_device(queries, keys, values, grad_out, frame_map, band, w_query, w_key, w_value, w_out):
    row_count = queries.shape[0]
    head_count = queries.shape[1] // HD
    frame_count = frame_map.shape[0]
    block_count = lax.axis_size("tm")
    score_scale = HD ** (-0.5)
    own_frame = frame_map[lax.axis_index("tm")]
    frame_ids = jnp.arange(frame_count, dtype=jnp.int32)
    slot_table = (frame_map[:, None] == frame_ids[None, :]).astype(jnp.int32)
    own_pick = (frame_ids == own_frame).astype(jnp.int32)
    band_row = jnp.sum(own_pick[:, None] * band, axis=0)
    out_by_slot = jnp.sum(slot_table * band_row[None, :], axis=1)
    positions = jnp.arange(row_count, dtype=jnp.int32)

    def pair_mask(count, by_slot):
        remote_pos = jnp.arange(count, dtype=jnp.int32)
        remote_inner = remote_pos % row_count
        slot_hit = (remote_pos // row_count)[:, None] == frame_ids[None, :]
        widths = jnp.sum(jnp.where(slot_hit, by_slot[None, :], 0), axis=1)
        return jnp.abs(positions[:, None] - remote_inner[None, :]) <= widths[None, :]

    d_flat = lax.dot_general(
        lax.all_gather(grad_out, "tensor", axis=1, tiled=True),
        w_out,
        (((1,), (1,)), ((), ())),
        preferred_element_type=jnp.float32,
    )
    d_output = d_flat.astype(jnp.bfloat16)
    query_heads = queries.reshape(row_count, head_count, HD)
    grad_heads = d_output.reshape(row_count, head_count, HD)
    forward_init = (
        jnp.full((head_count, row_count), masked_score, jnp.float32),
        jnp.zeros((head_count, row_count), jnp.float32),
        jnp.zeros((head_count, row_count, HD), jnp.float32),
    )
    pieces = (
        lax.all_gather(keys, "tm", axis=0, tiled=True),
        lax.all_gather(values, "tm", axis=0, tiled=True),
    )
    count = pieces[0].shape[0]
    key_piece = pieces[0].reshape(count, head_count, HD)
    value_piece = pieces[1].reshape(count, head_count, HD)
    allowed = pair_mask(count, out_by_slot)[None]

    def update(state):
        run_max, run_total, run_acc = state
        scores = (
            jnp.einsum("qhd,khd->hqk", query_heads, key_piece, preferred_element_type=jnp.float32)
            * score_scale
        )
        scores = jnp.where(allowed, scores, masked_score)
        new_max = jnp.maximum(run_max, jnp.max(scores, axis=2))
        shifted = jnp.where(allowed, jnp.exp(scores - new_max[..., None]), 0.0)
        new_total = jnp.sum(shifted, axis=2)
        new_acc = jnp.einsum(
            "hqk,khd->hqd",
            shifted.astype(jnp.bfloat16),
            value_piece,
            preferred_element_type=jnp.float32,
        )
        return (new_max, new_total, new_acc)

    run_max, run_total, run_acc = run_block(update, forward_init)
    log_total = run_max + jnp.log(run_total)
    attended = run_acc / run_total[..., None]
    row_dot = jnp.einsum("qhd,hqd->hq", grad_heads.astype(jnp.float32), attended)
    query_init = jnp.zeros((head_count, row_count, HD), jnp.float32)
    whole_init = jnp.zeros((row_count * block_count, head_count * HD), jnp.float32)
    backward_init = (query_init, whole_init, whole_init)
    pieces = (
        lax.all_gather(keys, "tm", axis=0, tiled=True),
        lax.all_gather(values, "tm", axis=0, tiled=True),
    )
    count = pieces[0].shape[0]
    backward_key_piece = pieces[0].reshape(count, head_count, HD)
    backward_value_piece = pieces[1].reshape(count, head_count, HD)
    backward_allowed = pair_mask(count, out_by_slot)[None]

    def update(state):
        probs_low, grad_scores = block_grads(
            query_heads,
            grad_heads,
            backward_key_piece,
            backward_value_piece,
            log_total,
            row_dot,
            backward_allowed,
            score_scale,
        )
        grad_query = (
            jnp.einsum(
                "hqk,khd->hqd", grad_scores, backward_key_piece, preferred_element_type=jnp.float32
            )
            * score_scale
        )
        key_term = (
            jnp.einsum("hqk,qhd->khd", grad_scores, query_heads, preferred_element_type=jnp.float32)
            * score_scale
        ).reshape(count, head_count * HD)
        value_term = jnp.einsum(
            "hqk,qhd->khd", probs_low, grad_heads, preferred_element_type=jnp.float32
        ).reshape(count, head_count * HD)
        result = (grad_query, key_term, value_term)
        return result

    backward_state = run_block(update, backward_init)
    grad_query_rows = (
        backward_state[0]
        .transpose(1, 0, 2)
        .reshape(row_count, head_count * HD)
        .astype(jnp.bfloat16)
    )
    key_sum, value_sum = (
        lax.psum_scatter(
            backward_state[1].astype(jnp.bfloat16), "tm", scatter_dimension=0, tiled=True
        ).astype(jnp.float32),
        lax.psum_scatter(
            backward_state[2].astype(jnp.bfloat16), "tm", scatter_dimension=0, tiled=True
        ).astype(jnp.float32),
    )
    grad_key_rows = key_sum.astype(jnp.bfloat16)
    grad_value_rows = value_sum.astype(jnp.bfloat16)
    total = jnp.zeros(
        (w_query.shape[0] // lax.axis_size("tensor") * lax.axis_size("tensor"), row_count),
        jnp.float32,
    )
    for weight, gradient in (
        (w_query, grad_query_rows),
        (w_key, grad_key_rows),
        (w_value, grad_value_rows),
    ):
        total = total + lax.dot_general(
            weight, gradient, (((1,), (1,)), ((), ())), preferred_element_type=jnp.float32
        )
    return lax.psum_scatter(total.astype(jnp.bfloat16), "tensor", scatter_dimension=0, tiled=True)


def solution(mesh):
    placed = (
        P("tm", "tensor"),
        P("tm", "tensor"),
        P("tm", "tensor"),
        P("tm", "tensor"),
        P(),
        P(),
        P(None, "tensor"),
        P(None, "tensor"),
        P(None, "tensor"),
        P("tensor", None),
    )
    return jax.shard_map(
        per_device, mesh=mesh, in_specs=placed, out_specs=P("tensor", "tm"), check_vma=False
    )
```

profile of v0, /device:TPU:0, one launch (start us, length us, event | category | flops | bytes accessed | tf_op | source)
XLA Modules:
  0.0 360.6 jit_solution(429837627555057352)
XLA Ops:
  6.5 2.0 copy.33
  8.6 0.7 all-gather.6.cloned.1.call-update
  9.4 1.9 copy.36
  11.4 1.3 dynamic_slice.3
  12.7 0.7 compare_convert_fusion
  13.4 0.8 multiply_reduce_fusion
  14.2 0.8 select_reduce_fusion.2
  15.0 1.2 copy.57
  16.2 0.1 select_reduce_fusion.1
  16.3 5.4 %abs_compare_fusion = pred[640,5120]{1,0:T(8,128)(4,1)} fusion(s32[5120]{0:T(1024)S(1)} %select_reduce_fusion.1, s32[5120]{0:T(1024)S(1)} %add_select_fusion.1), kind=kLoop, calls=%fused_computation.8 | loop fusion | flops 9830400 | bytes 3317760 | tf_op jit(solution)/shard_map/le | solution.py:51
  21.7 16.3 %all-gather.4.cloned.1.call-done = bf16[5120,256]{0,1:T(8,128)(2,1)} async-done(((bf16[640,256]{0,1:T(8,128)(2,1)}), bf16[5120,256]{0,1:T(8,128)(2,1)}) %all-gather.4.cloned.1.call-update) | async-done | bytes 2621456 | tf_op jit(solution)/shard_map/all_gather | solution.py:102
  38.0 14.1 %select_reduce_fusion = (f32[2,640]{1,0:T(2,128)S(1)}, f32[2,640,5120]{2,1,0:T(8,128)}) fusion(pred[640,5120]{1,0:T(8,128)(4,1)} %abs_compare_fusion, bf16[640,2,128]{0,2,1:T(8,128)(2,1)S(1)} %bitcast.40, bf16[5120,2,128]{0,2,1:T(8,128)(2,1)} %bitcast.43), kind=kOutput, calls=%fused_computation.3 | convolution fusion | flops 1697381120 | bytes 32445440 | tf_op jit(solution)/shard_map/qhd,khd->hqk/dot_general | solution.py:21
  52.1 14.6 %fusion.2 = f32[2,640]{1,0:T(2,128)S(1)} fusion(f32[2,640,5120]{2,1,0:T(8,128)} %get-tuple-element.6, f32[2,640]{1,0:T(2,128)S(1)} %broadcast_maximum_fusion, pred[640,5120]{1,0:T(8,128)(4,1)S(1)} %copy-done.1), kind=kLoop, calls=%fused_computation.6 | loop fusion | flops 32766720 | bytes 29501440 | tf_op jit(solution)/shard_map/reduce_sum | solution.py:85
  66.7 36.3 %all-gather.6.cloned.1.call-done = bf16[640,5120]{0,1:T(8,128)(2,1)} async-done(((bf16[640,320]{0,1:T(8,128)(2,1)}), bf16[640,5120]{0,1:T(8,128)(2,1)}) %all-gather.6.cloned.1.call-update) | async-done | bytes 6553616 | tf_op jit(solution)/shard_map/all_gather | solution.py:54
  103.0 5.9 %convolution_convert_fusion = bf16[640,256]{0,1:T(8,128)(2,1)S(1)} fusion(bf16[256,5120]{1,0:T(8,128)(2,1)} %param.19, bf16[640,5120]{0,1:T(8,128)(2,1)} %all-gather.6.cloned.1.call-done), kind=kOutput, calls=%fused_computation.18 | convolution fusion | flops 1677885440 | bytes 9502720 | tf_op jit(solution)/shard_map/dot_general | solution.py:53
  108.9 1.0 copy.50
  109.9 20.8 %all-gather.8.cloned.1.call-done = bf16[5120,256]{0,1:T(8,128)(2,1)} async-done(((bf16[640,256]{0,1:T(8,128)(2,1)}), bf16[5120,256]{0,1:T(8,128)(2,1)}) %all-gather.8.cloned.1.call-update) | async-done | bytes 2621456 | tf_op jit(solution)/shard_map/all_gather | solution.py:103
  130.7 13.7 %fusion.21 = f32[2,640]{1,0:T(2,128)S(1)} fusion(f32[2,640,128]{2,1,0:T(8,128)} %copy.50, bf16[5120,2,128]{0,2,1:T(8,128)(2,1)} %bitcast.49, f32[2,640,5120]{2,1,0:T(8,128)} %get-tuple-element.6, f32[2,640]{1,0:T(2,128)S(1)} %broadcast_maximum_fusion, pred[640,5120]{1,0:T(8,128)(4,1)} %abs_compare_fusion, f32[2,640]{1,0:T(2,128)S(1)} %fusion.2), kind=kOutput, calls=%fused_computation.22 | convolution fusion | flops 1710979840 | bytes 32783360 | tf_op jit(solution)/shard_map/hqk,khd->hqd/dot_general | solution.py:86
  144.4 20.6 %multiply_convert_fusion = bf16[2,640,5120]{2,1,0:T(8,128)(2,1)} fusion(f32[2,640,5120]{2,1,0:T(8,128)} %get-tuple-element.6, f32[2,640]{1,0:T(2,128)S(1)} %fusion.21, f32[2,640]{1,0:T(2,128)S(1)} %log_add_fusion, pred[640,5120]{1,0:T(8,128)(4,1)} %abs_compare_fusion, bf16[640,2,128]{0,2,1:T(8,128)(2,1)S(1)} %bitcast.47, bf16[5120,2,128]{0,2,1:T(8,128)(2,1)} %bitcast.50), kind=kOutput, calls=%fused_computation | convolution fusion | flops 1717043200 | bytes 45557760 | tf_op jit(solution)/shard_map/qhd,khd->hqk/dot_general | solution.py:25
  165.0 8.5 %fusion.10 = bf16[2,5120,128]{1,2,0:T(8,128)(2,1)} fusion(bf16[640,2,128]{0,2,1:T(8,128)(2,1)S(1)} %bitcast.41, bf16[2,640,5120]{2,1,0:T(8,128)(2,1)} %multiply_convert_fusion), kind=kOutput, calls=%fused_computation.15 | convolution fusion | flops 1680343040 | bytes 16056320 | tf_op jit(solution)/shard_map/hqk,qhd->khd/dot_general | solution.py:128
  173.5 4.4 %copy.51 = bf16[5120,256]{1,0:T(8,128)(2,1)} copy(bf16[5120,256]{0,1:T(8,128)(2,1)} %bitcast.39) | data formatting | bytes 5242880
  177.9 0.0 reduce-scatter.12.cloned.1.call-start
  177.9 14.3 %fusion.11 = bf16[2,128,5120]{2,1,0:T(8,128)(2,1)} fusion(bf16[640,2,128]{0,2,1:T(8,128)(2,1)S(1)} %bitcast.48, f32[2,640,5120]{2,1,0:T(8,128)} %get-tuple-element.6, f32[2,640]{1,0:T(2,128)S(1)} %log_add_fusion, pred[640,5120]{1,0:T(8,128)(4,1)} %abs_compare_fusion), kind=kOutput, calls=%fused_computation.16 | convolution fusion | flops 1705246720 | bytes 32445440 | tf_op jit(solution)/shard_map/hqk,qhd->khd/dot_general | solution.py:131
  192.2 4.4 %copy.53 = bf16[5120,256]{1,0:T(8,128)(2,1)} copy(bf16[5120,256]{0,1:T(8,128)(2,1)} %bitcast.42) | data formatting | bytes 5242880
  196.6 0.3 reduce-scatter.14.cloned.1.call-start
  196.9 9.8 %fusion.14 = bf16[2,640,128]{1,2,0:T(8,128)(2,1)S(1)} fusion(bf16[2,640,5120]{2,1,0:T(8,128)(2,1)} %multiply_convert_fusion, bf16[5120,2,128]{0,2,1:T(8,128)(2,1)} %bitcast.44), kind=kOutput, calls=%fused_computation.19 | convolution fusion | flops 1678049280 | bytes 16056320 | tf_op jit(solution)/shard_map/hqk,khd->hqd/dot_general | solution.py:122
  206.8 6.6 %fusion.34 = f32[640,5120]{1,0:T(8,128)} fusion(bf16[640,256]{0,1:T(8,128)(2,1)S(1)} %bitcast.45, bf16[5120,256]{1,0:T(8,128)(2,1)S(1)} %copy-done), kind=kOutput, calls=%fused_computation.46 | convolution fusion | flops 1677721600 | bytes 16056320 | tf_op jit(solution)/shard_map/dot_general | solution.py:163
  213.4 8.5 %fusion.35 = f32[640,5120]{1,0:T(8,128)} fusion(bf16[640,256]{1,0:T(8,128)(2,1)} %reduce-scatter.10.cloned.1.call-done, bf16[5120,256]{1,0:T(8,128)(2,1)} %param.17), kind=kOutput, calls=%fused_computation.47 | convolution fusion | flops 1677721600 | bytes 16056320 | tf_op jit(solution)/shard_map/dot_general | solution.py:163
  221.9 27.2 %reduce-scatter.12.cloned.1.call-done = bf16[640,256]{1,0:T(8,128)(2,1)} async-done(((bf16[5120,256]{1,0:T(8,128)(2,1)}), bf16[640,256]{1,0:T(8,128)(2,1)}) %reduce-scatter.12.cloned.1.call-update) | async-done | bytes 327696
  249.0 14.0 %fusion.9 = bf16[5120,640]{0,1:T(8,128)(2,1)} fusion(bf16[640,256]{1,0:T(8,128)(2,1)} %reduce-scatter.12.cloned.1.call-done, bf16[5120,256]{1,0:T(8,128)(2,1)} %param.18, f32[640,5120]{1,0:T(8,128)} %fusion.34, f32[640,5120]{1,0:T(8,128)} %fusion.35), kind=kOutput, calls=%fused_computation.13 | convolution fusion | flops 1687552000 | bytes 35717120 | tf_op jit(solution)/shard_map/dot_general | solution.py:163
  263.0 9.5 %copy.55 = bf16[5120,640]{1,0:T(8,128)(2,1)} copy(bf16[5120,640]{0,1:T(8,128)(2,1)} %fusion.9) | data formatting | bytes 13107200
  272.6 81.2 %reduce-scatter.14.cloned.1.call-done = bf16[320,640]{1,0:T(8,128)(2,1)} async-done(((bf16[5120,640]{1,0:T(8,128)(2,1)}), bf16[320,640]{1,0:T(8,128)(2,1)}) %reduce-scatter.14.cloned.1.call-update) | async-done | bytes 409616 | tf_op jit(solution)/shard_map/reduce_scatter | solution.py:166
  (18 shorter events, 0.3 us)
Async XLA Ops:
  6.5 200.2 %copy-start = (bf16[5120,256]{1,0:T(8,128)(2,1)S(1)}, bf16[5120,256]{1,0:T(8,128)(2,1)}, u32[]{:S(2)}) copy-start(bf16[5120,256]{1,0:T(8,128)(2,1)} %param.16) | copy-start | bytes 7864324
  6.5 31.4 %all-gather.4.cloned.1.call-start = ((), (), s32[]{:S(2)}) async-start(), calls=%async_computation.3 | async-start | bytes 2949120 | tf_op jit(solution)/shard_map/all_gather | solution.py:102
  8.6 94.4 %all-gather.6.cloned.1.call-start = ((), (), s32[]{:S(2)}) async-start(), calls=%async_computation.4 | async-start | bytes 6963200 | tf_op jit(solution)/shard_map/all_gather | solution.py:54
  9.3 121.4 %all-gather.8.cloned.1.call-start = ((), (), s32[]{:S(2)}) async-start(), calls=%async_computation.5 | async-start | bytes 2949120 | tf_op jit(solution)/shard_map/all_gather | solution.py:103
  11.3 202.1 %reduce-scatter.10.cloned.1.call-start = ((), (), s32[]{:S(2)}) async-start(), calls=%async_computation.6 | async-start | bytes 2949120
  38.0 14.1 %copy-start.1 = (pred[640,5120]{1,0:T(8,128)(4,1)S(1)}, pred[640,5120]{1,0:T(8,128)(4,1)}, u32[]{:S(2)}) copy-start(pred[640,5120]{1,0:T(8,128)(4,1)} %abs_compare_fusion) | copy-start | bytes 9830404
  177.9 71.1 %reduce-scatter.12.cloned.1.call-start = ((), (), s32[]{:S(2)}) async-start(), calls=%async_computation.7 | async-start | bytes 2949120
  196.6 157.1 %reduce-scatter.14.cloned.1.call-start = ((), (), s32[]{:S(2)}) async-start(), calls=%async_computation.8 | async-start | bytes 6963200 | tf_op jit(solution)/shard_map/reduce_scatter | solution.py:166
Sparse Core Ops, SparseCore 0:
  9.1 28.8 all-gather.3
  40.1 62.8 all-gather.5
  104.7 25.9 all-gather.7
  178.0 35.0 reduce-scatter.9
  215.4 33.5 reduce-scatter.11
  272.7 81.0 reduce-scatter.13
where the time goes:
time: 361 us
  waiting for transfers between devices  183 us (51%)
  matrix products  116 us (32%)
  local copies, waits for them, and re-layouts  25.7 us (7%)
  other arithmetic  22.5 us (6%)
  between operations  13.6 us (4%)
    reduce_scatter x1, waiting for transfers between devices, per_device(): lax.psum_scatter(total.astype(jnp.bfloat16), 'tensor', scatter_dimension=...  81.2 us
    all_gather x1, waiting for transfers between devices, per_device(): lax.all_gather(grad_out, 'tensor', axis=1, tiled=True)  36.3 us
    dot_general x3, matrix products, per_device(): lax.dot_general(weight, gradient, (((1,), (1,)), ((), ())), preferred_ele...  29.1 us
    unnamed x8, waiting for transfers between devices  27.9 us
    unnamed x10, local copies, waits for them, and re-layouts  23.2 us
    all_gather x1, waiting for transfers between devices, per_device(): lax.all_gather(values, 'tm', axis=0, tiled=True)  20.8 us
    dot_general x1, matrix products, block_grads(): jnp.einsum('qhd,khd->hqk', grad_piece, value_piece, preferred_element_typ...  20.6 us
    all_gather x1, waiting for transfers between devices, per_device(): lax.all_gather(keys, 'tm', axis=0, tiled=True)  16.3 us
  transfers between devices with their start and end apart: 6, of which 5 were waited for; matrix products, arithmetic and copies ran while one was open for 25% of the time, Pallas kernels for 0%

commit v1 on v0

v1 whole, which is shorter than its diff:
```python
import functools

import jax
import jax.numpy as jnp
from jax import lax
from jax.experimental import pallas as pl
from jax.experimental.pallas import tpu as pltpu
from jax.sharding import PartitionSpec as P

HD = 128
F = 640
MESH = pl.DeviceIdType.MESH
NT = (((1,), (1,)), ((), ()))
masked_score = -1e30


def dot(a, b):
    return jnp.dot(a, b, preferred_element_type=jnp.float32)


def dot_nt(a, b):
    return lax.dot_general(a, b, NT, preferred_element_type=jnp.float32)


def ring(position, step):
    return lax.rem(position + step + 4, 4)


def scatter_kernel(
    wq_hbm, wk_hbm, wv_hbm, gq_ref, gk_ref, gv_ref, out_ref,
    wq, wk, wv, gt, part, out1, in1, out2, in2, load_sem, s1, r1, s2, r2,
):
    g = lax.axis_index("tensor")
    z, x = g // 4, g % 4

    def block(half, d, e):
        zz = ring(z, d * (1 - half) + e * half)
        xx = ring(x, d * half + e * (1 - half))
        return zz * 4 + xx

    loads = [
        pltpu.make_async_copy(src, dst, load_sem.at[n])
        for n, (src, dst) in enumerate(((wq_hbm, wq), (wk_hbm, wk), (wv_hbm, wv)))
    ]
    for load in loads:
        load.start()
    barrier = pltpu.get_barrier_semaphore()
    for half in (0, 1):
        for step in (1, -1):
            pl.semaphore_signal(
                barrier, inc=1, device_id={"tensor": block(half, step, 0)}, device_id_type=MESH
            )
    for n, ref in enumerate((gq_ref, gk_ref, gv_ref)):
        gt[pl.ds(n * 256, 256), :] = ref[...].astype(jnp.float32).T.astype(jnp.bfloat16)
    for load in loads:
        load.wait()
    pl.semaphore_wait(barrier, 4)

    def first(m, half, step):
        return pltpu.make_async_remote_copy(
            src_ref=out1.at[m], dst_ref=in1.at[m], send_sem=s1.at[m], recv_sem=r1.at[m],
            device_id={"tensor": block(half, step, 0)}, device_id_type=MESH,
        )

    def second(m, half, step):
        return pltpu.make_async_remote_copy(
            src_ref=out2.at[m], dst_ref=in2.at[m], send_sem=s2.at[m], recv_sem=r2.at[m],
            device_id={"tensor": block(half, 0, step)}, device_id_type=MESH,
        )

    def body(i, carry):
        t, half = i // 2, i % 2
        group, u = t // 4, t % 4
        odd = u % 2
        own_only = (group % 2) * (1 - group // 2)
        par = (odd + own_only) % 2
        e = par * (1 - u // 2) + (1 - par) * (2 + u // 2)
        near = ((group + 1) // 2) % 2
        d = near * (1 + 2 * odd) + (1 - near) * (2 - 2 * (group // 3))
        row = pl.multiple_of(block(half, d, e) * 320 + half * 160, 16)
        rows = pl.ds(row, 160)
        part[...] = (
            dot(wq[rows, :], gt[0:256, :])
            + dot(wk[rows, :], gt[256:512, :])
            + dot(wv[rows, :], gt[512:768, :])
        )
        step = 1 - 2 * odd

        @pl.when(group < 2)
        def _():
            m = half * 12 + t
            out1[m] = part[...].astype(jnp.bfloat16)
            first(m, half, step).start()

        @pl.when(group == 2)
        def _():
            m = half * 12 + t
            first(m - 8, half, step).wait_recv()
            out1[m] = (part[...] + in1[m - 8].astype(jnp.float32)).astype(jnp.bfloat16)
            first(m, half, step).start()

        @pl.when(group == 3)
        def _():
            up = half * 12 + 8 - 4 * odd + 2 * (u // 2)
            down = half * 12 + 5 + 4 * odd + 2 * (u // 2)
            first(up, half, 1).wait_recv()
            first(down, half, 1).wait_recv()
            part[...] += in1[up].astype(jnp.float32) + in1[down].astype(jnp.float32)
            m = half * 6

            @pl.when(u == 0)
            def _():
                out2[m] = part[0:80, :].astype(jnp.bfloat16)
                second(m, half, 1).start()
                out2[m + 1] = part[80:160, :].astype(jnp.bfloat16)
                second(m + 1, half, -1).start()

            @pl.when(u == 1)
            def _():
                out2[m + 2] = part[80:160, :].astype(jnp.bfloat16)
                second(m + 2, half, 1).start()
                second(m, half, 1).wait_recv()
                out2[m + 3] = (part[0:80, :] + in2[m].astype(jnp.float32)).astype(jnp.bfloat16)
                second(m + 3, half, 1).start()

            @pl.when(u == 2)
            def _():
                out2[m + 4] = part[0:80, :].astype(jnp.bfloat16)
                second(m + 4, half, -1).start()
                second(m + 1, half, 1).wait_recv()
                out2[m + 5] = (part[80:160, :] + in2[m + 1].astype(jnp.float32)).astype(jnp.bfloat16)
                second(m + 5, half, -1).start()

            @pl.when(u == 3)
            def _():
                for n in (2, 3, 4, 5):
                    second(m + n, half, 1).wait_recv()
                at = pl.multiple_of(half * 160, 16)
                low = in2[m + 3].astype(jnp.float32) + in2[m + 4].astype(jnp.float32)
                high = in2[m + 2].astype(jnp.float32) + in2[m + 5].astype(jnp.float32)
                out_ref[pl.ds(at, 80), :] = (part[0:80, :] + low).astype(jnp.bfloat16)
                out_ref[pl.ds(at + 80, 80), :] = (part[80:160, :] + high).astype(jnp.bfloat16)

        return carry

    lax.fori_loop(0, 32, body, 0)

    def drain1(m, carry):
        first(m, 0, 1).wait_send()
        return carry

    def drain2(m, carry):
        second(m, 0, 1).wait_send()
        return carry

    lax.fori_loop(0, 24, drain1, 0)
    lax.fori_loop(0, 12, drain2, 0)


def weigh_and_scatter(w_query, w_key, w_value, gq, gk, gv):
    vmem = pl.BlockSpec(memory_space=pltpu.VMEM)
    hbm = pl.BlockSpec(memory_space=pl.ANY)
    weight = pltpu.VMEM((5120, 256), jnp.bfloat16)
    return pl.pallas_call(
        scatter_kernel,
        out_shape=jax.ShapeDtypeStruct((320, F), jnp.bfloat16),
        in_specs=[hbm] * 3 + [vmem] * 3,
        out_specs=vmem,
        scratch_shapes=[
            weight, weight, weight,
            pltpu.VMEM((768, F), jnp.bfloat16),
            pltpu.VMEM((160, F), jnp.float32),
            pltpu.VMEM((24, 160, F), jnp.bfloat16),
            pltpu.VMEM((24, 160, F), jnp.bfloat16),
            pltpu.VMEM((12, 80, F), jnp.bfloat16),
            pltpu.VMEM((12, 80, F), jnp.bfloat16),
            pltpu.SemaphoreType.DMA((3,)),
            pltpu.SemaphoreType.DMA((24,)),
            pltpu.SemaphoreType.DMA((24,)),
            pltpu.SemaphoreType.DMA((12,)),
            pltpu.SemaphoreType.DMA((12,)),
        ],
        compiler_params=pltpu.CompilerParams(
            collective_id=1, has_side_effects=True, vmem_limit_bytes=48 * 1024 * 1024
        ),
        cost_estimate=pl.CostEstimate(flops=5_033_164_800, bytes_accessed=9_000_000, transcendentals=0),
    )(w_query, w_key, w_value, gq, gk, gv)


SCALE = HD ** -0.5
POWER = SCALE * 1.4426950408889634
ARRAYS = 6


def attend_kernel(
    frame_map, band, go_hbm, wo_hbm, q_hbm, k_hbm, v_hbm, gq_out, gk_out, gv_out,
    go, wo, wt, qall, kall, vall, dall, logs, dots, p, pt, sbuf, dist, dacc, att, gq, gk, gv,
    inv_total, row_dot, load_sem, zs, zr, ys, yr,
):
    g = lax.axis_index("tensor")
    z, x = g // 4, g % 4
    me = lax.axis_index("tm")
    y, core = me // 2, me % 2
    my_frame = frame_map[me]

    loads = [
        pltpu.make_async_copy(src, dst, load_sem.at[n])
        for n, (src, dst) in enumerate((
            (go_hbm, go.at[g]), (k_hbm, kall.at[me]), (q_hbm, qall.at[me]), (v_hbm, vall.at[me]),
            (wo_hbm, wo),
        ))
    ]
    for load in loads:
        load.start()

    def block(half, d, e):
        zz = ring(z, d * half + e * (1 - half))
        xx = ring(x, d * (1 - half) + e * half)
        return zz * 4 + xx

    def piece(half, j, kind):
        start = half * 320 + (160 if kind == 3 else 0)
        return go.at[j, pl.ds(pl.multiple_of(start, 32), 320 if kind < 2 else 160)]

    def tensor_copy(half, m, j, kind, target):
        ref = piece(half, j, kind)
        n = half * 20 + m
        return pltpu.make_async_remote_copy(
            src_ref=ref, dst_ref=ref, send_sem=zs.at[n], recv_sem=zr.at[n],
            device_id={"tensor": target}, device_id_type=MESH,
        )

    def both(step):
        def one(half, carry):
            step(half)
            return carry

        lax.fori_loop(0, 2, one, 0)

    def spread(half, index, d):
        j = block(half, d, 0)
        m = 4 + 4 * index
        tensor_copy(half, m, j, 0, block(half, 0, 1)).start()
        tensor_copy(half, m + 1, j, 1, block(half, 0, -1)).start()

    def tensor_start(half):
        tensor_copy(half, 0, g, 0, block(half, 1, 0)).start()
        tensor_copy(half, 1, g, 1, block(half, -1, 0)).start()
        spread(half, 0, 0)

    def tensor_near(half):
        j = block(half, -1, 0)
        tensor_copy(half, 0, j, 0, g).wait_recv()
        tensor_copy(half, 2, j, 2, block(half, 1, 0)).start()
        spread(half, 1, -1)
        j = block(half, 1, 0)
        tensor_copy(half, 1, j, 1, g).wait_recv()
        tensor_copy(half, 3, j, 3, block(half, -1, 0)).start()
        spread(half, 2, 1)

    def tensor_far(half):
        j = block(half, 2, 0)
        tensor_copy(half, 2, j, 2, g).wait_recv()
        tensor_copy(half, 3, j, 3, g).wait_recv()
        spread(half, 3, 2)

    offsets = (0, -1, 1, 2)

    def forward(index):
        def step(half):
            m, d = 4 + 4 * index, offsets[index]
            j = block(half, d, -1)
            tensor_copy(half, m, j, 0, g).wait_recv()
            tensor_copy(half, m + 2, j, 2, block(half, 0, 1)).start()
            j = block(half, d, 1)
            tensor_copy(half, m + 1, j, 1, g).wait_recv()
            tensor_copy(half, m + 3, j, 3, block(half, 0, -1)).start()

        both(step)

    def finish(index):
        def step(half):
            m, d = 4 + 4 * index, offsets[index]
            j = block(half, d, 2)
            tensor_copy(half, m + 2, j, 2, g).wait_recv()
            tensor_copy(half, m + 3, j, 3, g).wait_recv()

        both(step)

        def add(i, carry):
            half = i // 4
            j = block(half, offsets[index], i % 4)
            rows = pl.ds(pl.multiple_of(half * 320, 64), 320)
            dacc[rows, :] += dot_nt(go[j, rows, :], wt[j])
            return carry

        lax.fori_loop(0, 8, add, 0)

    sibling = y * 2 + 1 - core

    def at_y(step):
        return ring(y, step) * 2 + core

    def tm_copy(array, ref, m, slot, target):
        half = ref.shape[1] // 2
        part = ref.at[slot]
        if m in (2, 3):
            part = ref.at[slot, pl.ds((m - 2) * half, half)]
        n = array * 8 + m
        return pltpu.make_async_remote_copy(
            src_ref=part, dst_ref=part, send_sem=ys.at[n], recv_sem=yr.at[n],
            device_id={"tm": target}, device_id_type=MESH,
        )

    def tm_start(array, ref):
        tm_copy(array, ref, 0, me, at_y(1)).start()
        tm_copy(array, ref, 1, me, at_y(-1)).start()
        tm_copy(array, ref, 4, me, sibling).start()

    def tm_near(array, ref):
        tm_copy(array, ref, 0, at_y(-1), me).wait_recv()
        tm_copy(array, ref, 2, at_y(-1), at_y(1)).start()
        tm_copy(array, ref, 5, at_y(-1), sibling).start()
        tm_copy(array, ref, 1, at_y(1), me).wait_recv()
        tm_copy(array, ref, 3, at_y(1), at_y(-1)).start()
        tm_copy(array, ref, 6, at_y(1), sibling).start()

    def tm_far(array, ref):
        tm_copy(array, ref, 2, at_y(2), me).wait_recv()
        tm_copy(array, ref, 3, at_y(2), me).wait_recv()
        tm_copy(array, ref, 7, at_y(2), sibling).start()

    def tm_finish(array, ref):
        for m, step in ((4, 0), (5, -1), (6, 1), (7, 2)):
            slot = ring(y, step) * 2 + 1 - core
            tm_copy(array, ref, m, slot, me).wait_recv()

    keys, queries, values, grads, totals, products = range(ARRAYS)

    def lanes(h):
        return pl.ds(pl.multiple_of(h * HD, HD), HD)

    def stat_row(ref, s, h):
        return ref[s, pl.ds(pl.multiple_of(h * 8, 8), 8), :][0:1, :]

    def to_row(ref, h, column):
        wide = jnp.broadcast_to(column, (F, HD))
        ref[me, h * 8:(h + 1) * 8, :] = wide.T[0:8, :]

    def softmax(i, carry):
        h = i // 2
        rows = pl.ds(pl.multiple_of((i % 2) * 320, 64), 320)
        query = qall[me, rows, lanes(h)]

        def score(s, top):
            scores = dot_nt(query, kall[s, :, lanes(h)])
            width = band[my_frame, frame_map[s]]
            scores = jnp.where(dist[rows, :] <= width, scores, masked_score)
            sbuf[s] = scores
            for n in range(5):
                top = jnp.maximum(top, scores[:, n * 128:(n + 1) * 128])
            return top

        top = lax.fori_loop(0, 8, score, jnp.full((320, 128), masked_score, jnp.float32))
        top = jnp.max(top, axis=1, keepdims=True) * POWER

        def weigh(s, total):
            shifted = jnp.exp2(sbuf[s] * POWER - top)
            p[h, s, rows, :] = shifted.astype(jnp.bfloat16)
            for n in range(5):
                total = total + shifted[:, n * 128:(n + 1) * 128]
            return total

        total = lax.fori_loop(0, 8, weigh, jnp.zeros((320, 128), jnp.float32))
        total = jnp.sum(total, axis=1, keepdims=True)
        inv_total[h, rows, :] = jnp.broadcast_to(1.0 / total, (320, HD))
        row_dot[h, rows, :] = jnp.broadcast_to(top + jnp.log2(total), (320, HD))
        return carry

    def key_side(i, carry):
        h, s = i // 16, (i // 2) % 8
        rows = pl.ds(pl.multiple_of((i % 2) * 320, 64), 320)
        scores = dot_nt(kall[me, rows, lanes(h)], qall[s, :, lanes(h)])
        width = band[frame_map[s], my_frame]
        power = jnp.where(
            dist[rows, :] <= width, scores * POWER - stat_row(logs, s, h), masked_score
        )
        pt[h, s, rows, :] = jnp.exp2(power).astype(jnp.bfloat16)
        return carry

    def attend(i, carry):
        h, s = i // 8, i % 8
        att[h] += dot(p[h, s], vall[s, :, lanes(h)])
        return carry

    def query_grad(i, carry):
        h, s = i // 16, (i // 2) % 8
        rows = pl.ds(pl.multiple_of((i % 2) * 320, 64), 320)
        grad = dot_nt(dall[me, rows, lanes(h)], vall[s, :, lanes(h)])
        weight = p[h, s, rows, :].astype(jnp.float32)
        grad = weight * ((grad - row_dot[h, rows, 0:1]) * inv_total[h, rows, 0:1])
        gq[h, rows, :] += dot(grad.astype(jnp.bfloat16), kall[s, :, lanes(h)])
        return carry

    def key_grad(i, carry):
        h, s = i // 16, (i // 2) % 8
        rows = pl.ds(pl.multiple_of((i % 2) * 320, 64), 320)
        grad_rows = dall[s, :, lanes(h)]
        weight = pt[h, s, rows, :]
        grad = dot_nt(vall[me, rows, lanes(h)], grad_rows)
        grad = weight.astype(jnp.float32) * (grad - stat_row(dots, s, h))
        gv[h, rows, :] += dot(weight, grad_rows)
        gk[h, rows, :] += dot(grad.astype(jnp.bfloat16), qall[s, :, lanes(h)])
        return carry

    barrier = pltpu.get_barrier_semaphore()
    for half in (0, 1):
        for step in (1, -1):
            pl.semaphore_signal(
                barrier, inc=1, device_id={"tensor": block(half, step, 0)}, device_id_type=MESH
            )
    for target in (at_y(1), at_y(-1), sibling):
        pl.semaphore_signal(barrier, inc=1, device_id={"tm": target}, device_id_type=MESH)
    loads[0].wait()
    loads[1].wait()
    pl.semaphore_wait(barrier, 7)
    both(tensor_start)
    tm_start(keys, kall)
    across = lax.broadcasted_iota(jnp.int32, (F, F), 0) - lax.broadcasted_iota(jnp.int32, (F, F), 1)
    dist[...] = jnp.abs(across)
    for ref in (dacc, att, gq, gk, gv):
        ref[...] = jnp.zeros_like(ref)
    loads[2].wait()
    loads[3].wait()
    loads[4].wait()
    both(tensor_near)
    tm_near(keys, kall)
    tm_start(queries, qall)
    for j in range(16):
        wt[j] = wo[:, j * 320:(j + 1) * 320]
    both(tensor_far)
    tm_far(keys, kall)
    tm_finish(keys, kall)
    lax.fori_loop(0, 1, softmax, 0)
    forward(0)
    tm_near(queries, qall)
    tm_start(values, vall)
    lax.fori_loop(1, 3, softmax, 0)
    forward(1)
    tm_far(queries, qall)
    lax.fori_loop(3, 4, softmax, 0)
    for h in (0, 1):
        to_row(logs, h, row_dot[h, :, 0:1])
    tm_start(totals, logs)
    forward(2)
    tm_near(values, vall)
    tm_near(totals, logs)
    tm_finish(queries, qall)
    finish(0)
    tm_far(totals, logs)
    tm_finish(totals, logs)
    lax.fori_loop(0, 16, key_side, 0)
    forward(3)
    tm_far(values, vall)
    finish(1)
    lax.fori_loop(16, 32, key_side, 0)
    tm_finish(values, vall)
    lax.fori_loop(0, 16, attend, 0)
    finish(2)
    finish(3)

    dall[me] = dacc[...].astype(jnp.bfloat16)
    tm_start(grads, dall)
    for h in (0, 1):
        grad_rows = dall[me, :, h * HD:(h + 1) * HD].astype(jnp.float32)
        column = jnp.sum(grad_rows * att[h], axis=1, keepdims=True) * inv_total[h, :, 0:1]
        row_dot[h] = jnp.broadcast_to(column, (F, HD))
        to_row(dots, h, column)
    tm_start(products, dots)
    lax.fori_loop(0, 20, query_grad, 0)
    tm_near(grads, dall)
    tm_near(products, dots)
    lax.fori_loop(20, 32, query_grad, 0)
    tm_far(grads, dall)
    tm_far(products, dots)
    for h in (0, 1):
        gq_out[:, h * HD:(h + 1) * HD] = (gq[h] * SCALE).astype(jnp.bfloat16)
    tm_finish(grads, dall)
    tm_finish(products, dots)
    lax.fori_loop(0, 32, key_grad, 0)
    for h in (0, 1):
        gk_out[:, h * HD:(h + 1) * HD] = (gk[h] * SCALE).astype(jnp.bfloat16)
        gv_out[:, h * HD:(h + 1) * HD] = gv[h].astype(jnp.bfloat16)

    def drain(half):
        def one(i, carry):
            for kind in range(4):
                tensor_copy(half, 4 * i + kind, g, kind, g).wait_send()
            return carry

        lax.fori_loop(0, 5, one, 0)

    both(drain)
    gathered = (kall, qall, vall, dall, logs, dots)
    for array, ref in enumerate(gathered):
        for m in range(8):
            tm_copy(array, ref, m, me, me).wait_send()


def attend(frame_map, band, grad_out, w_out, queries, keys, values):
    vmem = pl.BlockSpec(memory_space=pltpu.VMEM)
    hbm = pl.BlockSpec(memory_space=pl.ANY)
    smem = pl.BlockSpec(memory_space=pltpu.SMEM)
    grad = jax.ShapeDtypeStruct((F, 256), jnp.bfloat16)
    gathered = pltpu.VMEM((8, F, 256), jnp.bfloat16)
    stats = pltpu.VMEM((8, 16, F), jnp.float32)
    pairs = pltpu.VMEM((2, 8, F, F), jnp.bfloat16)
    heads = pltpu.VMEM((2, F, HD), jnp.float32)
    return pl.pallas_call(
        attend_kernel,
        out_shape=(grad, grad, grad),
        in_specs=[smem] * 2 + [hbm] * 5,
        out_specs=(vmem, vmem, vmem),
        scratch_shapes=[
            pltpu.VMEM((16, F, 320), jnp.bfloat16),
            pltpu.VMEM((256, 5120), jnp.bfloat16),
            pltpu.VMEM((16, 256, 320), jnp.bfloat16),
            gathered, gathered, gathered, gathered,
            stats, stats,
            pairs, pairs,
            pltpu.VMEM((8, 320, F), jnp.float32),
            pltpu.VMEM((F, F), jnp.int32),
            pltpu.VMEM((F, 256), jnp.float32),
            heads, heads, heads, heads, heads, heads,
            pltpu.SemaphoreType.DMA((5,)),
            pltpu.SemaphoreType.DMA((40,)),
            pltpu.SemaphoreType.DMA((40,)),
            pltpu.SemaphoreType.DMA((8 * ARRAYS,)),
            pltpu.SemaphoreType.DMA((8 * ARRAYS,)),
        ],
        compiler_params=pltpu.CompilerParams(
            collective_id=0, has_side_effects=True, vmem_limit_bytes=64 * 1024 * 1024
        ),
        cost_estimate=pl.CostEstimate(
            flops=16_000_000_000, bytes_accessed=6_000_000, transcendentals=13_000_000
        ),
    )(frame_map, band, grad_out, w_out, queries, keys, values)


def per_device(queries, keys, values, grad_out, frame_map, band, w_query, w_key, w_value, w_out):
    gq, gk, gv = attend(frame_map, band, grad_out, w_out, queries, keys, values)
    return weigh_and_scatter(w_query, w_key, w_value, gq, gk, gv)


def solution(mesh):
    placed = (
        P("tm", "tensor"),
        P("tm", "tensor"),
        P("tm", "tensor"),
        P("tm", "tensor"),
        P(),
        P(),
        P(None, "tensor"),
        P(None, "tensor"),
        P(None, "tensor"),
        P("tensor", None),
    )
    return jax.shard_map(
        per_device, mesh=mesh, in_specs=placed, out_specs=P("tensor", "tm"), check_vma=False
    )
```

time: 361 us -> 171 us (0.47)
  waiting for transfers between devices: 183 us -> 0 us
  Pallas kernels: 0 us -> 162 us
  matrix products: 116 us -> 0 us
  other arithmetic: 22.5 us -> 0 us
  local copies, waits for them, and re-layouts: 25.7 us -> 7.39 us
  between operations: 13.6 us -> 0.03 us
    pallas_call x0 -> x2, Pallas kernels: none -> 162 us  [the longest x1 119 us: attend(): pl.pallas_call(attend_kernel, out_shape=(grad, grad, grad), in_specs=[sme...]
    dot_general x10 -> x0, matrix products: 116 us -> none  [the longest x3 29.1 us: per_device(): lax.dot_general(weight, gradient, (((1,), (1,)), ((), ())), preferred_ele...]
    reduce_scatter x1 -> x0, waiting for transfers between devices: 81.2 us -> none  [per_device(): lax.psum_scatter(total.astype(jnp.bfloat16), 'tensor', scatter_dimension=...]
    all_gather x3 -> x0, waiting for transfers between devices: 73.4 us -> none  [the longest x1 36.3 us: per_device(): lax.all_gather(grad_out, 'tensor', axis=1, tiled=True)]
    unnamed x8 -> x0, waiting for transfers between devices: 27.9 us -> none
    reduce_sum x4 -> x0, other arithmetic: 16.3 us -> none  [the longest x1 14.6 us: update(): new_total = jnp.sum(shifted, axis=2)]
    unnamed x10, local copies, waits for them, and re-layouts: 23.2 us -> 7.39 us
    le x1 -> x0, other arithmetic: 5.4 us -> none  [pair_mask(): jnp.abs(positions[:, None] - remote_inner[None, :]) <= widths[None, :]]
  transfers between devices with their start and end apart: 6 -> 0, of which waited for: 5 -> 0; matrix products, arithmetic and copies ran while one was open for 25% -> 0% of each run, Pallas kernels for 0% -> 0%
where the time goes in v1:
time: 171 us; the launch traced here: 170 us
  Pallas kernels  162 us (95%)
  local copies, waits for them, and re-layouts  7.39 us (4%)
    pallas_call x1, Pallas kernels, attend(): pl.pallas_call(attend_kernel, out_shape=(grad, grad, grad), in_specs=[sme...  119 us
    pallas_call x1, Pallas kernels, weigh_and_scatter(): pl.pallas_call(scatter_kernel, out_shape=jax.ShapeDtypeStruct((320, F), j...  43.9 us
    unnamed x10, local copies, waits for them, and re-layouts  7.39 us

profile of v1, /device:TPU:0, one launch (start us, length us, event | category | flops | bytes accessed | tf_op | source)
XLA Modules:
  0.0 169.9 jit_solution(11862836781780944687)
XLA Ops:
  0.0 2.0 %copy.11.go_hbm = bf16[640,320]{1,0:T(8,128)(2,1)} copy(bf16[640,320]{0,1:T(8,128)(2,1)} %param.13) | data formatting | bytes 819200 | tf_op args[3]
  2.0 118.6 %shard_map.100 = (bf16[640,256]{1,0:T(8,128)(2,1)}, bf16[640,256]{1,0:T(8,128)(2,1)}, bf16[640,256]{1,0:T(8,128)(2,1)}) custom-call(s32[8]{0:T(128)} %frame_map.1, s32[8,8]{1,0:T(8,128)} %band.1, bf16[640,320]{1,0:T(8,128)(2,1)} %copy.11.go_hbm, bf16[256,5120]{1,0:T(8,128)(2,1)} %wo_hbm.1, bf16[640,256]{1,0:T(8,128)(2,1)} %q_hbm.1, bf16[640,256]{1,0:T(8,128)(2,1)} %k_hbm.1, ...), custom_call_target="tpu_custom_call" | custom-call | flops 16000000000 | bytes 6000000 | tf_op jit(solution)/shard_map/pallas_call | solution.py:519
  120.6 0.0 copy-start
  120.6 1.7 %copy-done = bf16[5120,256]{1,0:T(8,128)(2,1)S(1)} copy-done((bf16[5120,256]{1,0:T(8,128)(2,1)S(1)}, bf16[5120,256]{1,0:T(8,128)(2,1)}, u32[]{:S(2)}) %copy-start) | copy-done | bytes 2621464
  122.3 0.0 copy-start.1
  122.3 1.0 copy-done.1
  123.3 0.0 copy-start.2
  123.3 1.0 copy-done.2
  124.2 0.0 copy-start.3
  124.2 1.0 copy-done.3
  125.2 43.9 %shard_map.101 = bf16[320,640]{1,0:T(8,128)(2,1)S(1)} custom-call(bf16[5120,256]{1,0:T(8,128)(2,1)S(1)} %copy-done, bf16[5120,256]{1,0:T(8,128)(2,1)} %wk_hbm.1, bf16[5120,256]{1,0:T(8,128)(2,1)} %wv_hbm.1, bf16[640,256]{1,0:T(8,128)(2,1)S(1)} %copy-done.1, bf16[640,256]{1,0:T(8,128)(2,1)S(1)} %copy-done.2, bf16[640,256]{1,0:T(8,128)(2,1)S(1)} %copy-done.3), custom_call_target="tpu_custom_call" | custom-call | flops 5033164800 | bytes 9000000 | tf_op jit(solution)/shard_map/pallas_call | solution.py:164
  169.1 0.8 copy.13
Async XLA Ops:
  120.6 1.7 %copy-start = (bf16[5120,256]{1,0:T(8,128)(2,1)S(1)}, bf16[5120,256]{1,0:T(8,128)(2,1)}, u32[]{:S(2)}) copy-start(bf16[5120,256]{1,0:T(8,128)(2,1)} %wq_hbm.1) | copy-start | bytes 7864324
  122.3 1.0 copy-start.1
  123.3 1.0 copy-start.2
  124.2 1.0 copy-start.3

commit v2 on v0

v2 whole, which is shorter than its diff:
```python
import jax
import jax.numpy as jnp
from jax import lax
from jax.experimental import pallas as pl
from jax.experimental.pallas import tpu as pltpu
from jax.sharding import PartitionSpec as P

HD = 128
F = 640
SCALE = HD ** -0.5
POWER = SCALE * 1.4426950408889634
ARRAYS = 6
MESH = pl.DeviceIdType.MESH
NT = (((1,), (1,)), ((), ()))
masked_score = -1e30


def dot(a, b):
    return jnp.dot(a, b, preferred_element_type=jnp.float32)


def dot_nt(a, b):
    return lax.dot_general(a, b, NT, preferred_element_type=jnp.float32)


def ring(position, step):
    return lax.rem(position + step + 4, 4)


def low(value):
    return value.astype(jnp.bfloat16)


def wide(value):
    return value.astype(jnp.float32)


def kernel(
    frame_map, band, go_hbm, wo_hbm, q_hbm, k_hbm, v_hbm, wq_hbm, wk_hbm, wv_hbm, out_ref,
    go, wo, wq, kall, qall, vall, dall, vown, logs, dots, p, pt, dist, dacc, att, gq, gk, gv,
    tops, sums, row_dot, part, in1, in2,
    load_sem, zs, zr, ys, yr, s1, r1, s2, r2,
):
    g = lax.axis_index("tensor")
    z, x = g // 4, g % 4
    me = lax.axis_index("tm")
    y, core = me // 2, me % 2
    my_frame = frame_map[me]

    def slot_rows(s):
        return pl.ds(pl.multiple_of(s * F, F), F)

    mine = slot_rows(me)

    def load(n, src, dst):
        return pltpu.make_async_copy(src, dst, load_sem.at[n])

    loads = [
        load(0, go_hbm, go.at[pl.ds(pl.multiple_of(g * 320, 320), 320)]),
        load(1, k_hbm, kall.at[mine]),
        load(2, q_hbm, qall.at[mine]),
        load(3, v_hbm, vall.at[mine]),
        load(4, v_hbm, vown),
        load(5, wo_hbm, wo),
        load(6, wq_hbm, wq),
    ]
    for item in loads:
        item.start()

    def block(half, d, e):
        zz = ring(z, d * half + e * (1 - half))
        xx = ring(x, d * (1 - half) + e * half)
        return zz * 4 + xx

    def tensor_copy(half, m, j, kind, target):
        start = j * 320 + half * 160 + (80 if kind == 3 else 0)
        ref = go.at[pl.ds(pl.multiple_of(start, 16), 160 if kind < 2 else 80)]
        n = half * 20 + m
        return pltpu.make_async_remote_copy(
            src_ref=ref, dst_ref=ref, send_sem=zs.at[n], recv_sem=zr.at[n],
            device_id={"tensor": target}, device_id_type=MESH,
        )

    def both(step):
        def one(half, carry):
            step(half)
            return carry

        lax.fori_loop(0, 2, one, 0)

    def spread(half, index, d):
        j = block(half, d, 0)
        m = 4 + 4 * index
        tensor_copy(half, m, j, 0, block(half, 0, 1)).start()
        tensor_copy(half, m + 1, j, 1, block(half, 0, -1)).start()

    def tensor_start(half):
        tensor_copy(half, 0, g, 0, block(half, 1, 0)).start()
        tensor_copy(half, 1, g, 1, block(half, -1, 0)).start()

    def tensor_next(half):
        spread(half, 0, 0)

    def tensor_near(half):
        j = block(half, -1, 0)
        tensor_copy(half, 0, j, 0, g).wait_recv()
        tensor_copy(half, 2, j, 2, block(half, 1, 0)).start()
        spread(half, 1, -1)
        j = block(half, 1, 0)
        tensor_copy(half, 1, j, 1, g).wait_recv()
        tensor_copy(half, 3, j, 3, block(half, -1, 0)).start()
        spread(half, 2, 1)

    def tensor_far(half):
        j = block(half, 2, 0)
        tensor_copy(half, 2, j, 2, g).wait_recv()
        tensor_copy(half, 3, j, 3, g).wait_recv()
        spread(half, 3, 2)

    offsets = (0, -1, 1, 2)

    def forward(index):
        def step(half):
            m, d = 4 + 4 * index, offsets[index]
            j = block(half, d, -1)
            tensor_copy(half, m, j, 0, g).wait_recv()
            tensor_copy(half, m + 2, j, 2, block(half, 0, 1)).start()
            j = block(half, d, 1)
            tensor_copy(half, m + 1, j, 1, g).wait_recv()
            tensor_copy(half, m + 3, j, 3, block(half, 0, -1)).start()

        both(step)

    def finish(half, index):
        m, d = 4 + 4 * index, offsets[index]
        j = block(half, d, 2)
        tensor_copy(half, m + 2, j, 2, g).wait_recv()
        tensor_copy(half, m + 3, j, 3, g).wait_recv()

    def add_row(index):
        cols = pl.ds(pl.multiple_of(ring(z, offsets[index]) * 1280, 1280), 1280)
        dacc[...] += dot(wo[:, cols], go[cols, :])

    sibling = y * 2 + 1 - core

    def at_y(step):
        return ring(y, step) * 2 + core

    class Gather:
        def __init__(self, array, ref, rows):
            self.array, self.ref, self.rows = array, ref, rows

        def copy(self, m, slot, target):
            start, count = slot * self.rows, self.rows
            if m in (2, 3):
                count = self.rows // 2
                start = start + (m - 2) * count
            ref = self.ref.at[pl.ds(pl.multiple_of(start, count), count)]
            n = self.array * 8 + m
            return pltpu.make_async_remote_copy(
                src_ref=ref, dst_ref=ref, send_sem=ys.at[n], recv_sem=yr.at[n],
                device_id={"tm": target}, device_id_type=MESH,
            )

        def start(self):
            self.copy(0, me, at_y(1)).start()
            self.copy(1, me, at_y(-1)).start()
            self.copy(4, me, sibling).start()

        def near(self):
            self.copy(0, at_y(-1), me).wait_recv()
            self.copy(2, at_y(-1), at_y(1)).start()
            self.copy(5, at_y(-1), sibling).start()
            self.copy(1, at_y(1), me).wait_recv()
            self.copy(3, at_y(1), at_y(-1)).start()
            self.copy(6, at_y(1), sibling).start()

        def far(self):
            self.copy(2, at_y(2), me).wait_recv()
            self.copy(3, at_y(2), me).wait_recv()
            self.copy(7, at_y(2), sibling).start()

        def from_sibling(self, *messages):
            for m in messages:
                slot = ring(y, (0, -1, 1, 2)[m - 4]) * 2 + 1 - core
                self.copy(m, slot, me).wait_recv()

        def drain(self):
            for m in range(8):
                self.copy(m, me, me).wait_send()

    keys, queries = Gather(0, kall, F), Gather(1, qall, F)
    values, grads = Gather(2, vall, F), Gather(3, dall, F)
    totals, products = Gather(4, logs, 16), Gather(5, dots, 16)

    def by_arrival(gathers, body, events):
        def step(n, carry):
            ring_at = (n + 2) // 4
            hop = (ring_at % 2) * (2 * (n % 2) - 1) + (ring_at // 2) * 2
            other = (1 - ring_at % 2) * (n % 2) + (ring_at % 2) * (((n + 2) // 2) % 2)
            slot = ring(y, hop) * 2 + (core + other) % 2
            waits = {
                1: lambda item: item.from_sibling(4),
                4: lambda item: item.from_sibling(5, 6),
                6: lambda item: item.far(),
                7: lambda item: item.from_sibling(7),
            }
            for when in range(8):
                if when in waits or when in events:
                    @pl.when(n == when)
                    def _(when=when):
                        if when in events:
                            events[when]()
                        if when in waits:
                            for item in gathers:
                                waits[when](item)

            body(slot)
            return carry

        lax.fori_loop(0, 8, step, 0)

    lane = lax.broadcasted_iota(jnp.int32, (F, HD), 1)

    def head(ref, rows, h):
        return ref[rows, h * HD:(h + 1) * HD]

    def stat_row(ref, s, h):
        return ref[pl.ds(pl.multiple_of(s * 16 + h * 8, 8), 8), :][0:1, :]

    def to_row(ref, h, column):
        rows = pl.ds(pl.multiple_of(me * 16 + h * 8, 8), 8)
        ref[rows, :] = jnp.broadcast_to(column, (F, HD)).T[0:8, :]

    def factor(h, s):
        return jnp.sum(jnp.where(lane == s, sums[h], 0.0), axis=1, keepdims=True)

    def softmax(s):
        width = band[my_frame, frame_map[s]]
        for h in (0, 1):
            scores = dot_nt(head(qall, mine, h), head(kall, slot_rows(s), h))
            scores = jnp.where(dist[...] <= width, scores, masked_score)
            top = jnp.max(scores, axis=1, keepdims=True) * POWER
            shifted = jnp.exp2(scores * POWER - top)
            total = jnp.sum(shifted, axis=1, keepdims=True)
            p[h, s] = low(shifted)
            tops[h] = jnp.where(lane == s, top, tops[h])
            sums[h] = jnp.where(lane == s, total, sums[h])

    def combine():
        for h in (0, 1):
            top = jnp.max(tops[h], axis=1, keepdims=True)
            shares = jnp.exp2(tops[h] - top)
            total = jnp.sum(shares * sums[h], axis=1, keepdims=True)
            sums[h] = shares / total
            to_row(logs, h, top + jnp.log2(total))

    def key_side(s):
        width = band[frame_map[s], my_frame]
        for h in (0, 1):
            scores = dot_nt(head(kall, mine, h), head(qall, slot_rows(s), h))
            power = jnp.where(
                dist[...] <= width, scores * POWER - stat_row(logs, s, h), masked_score
            )
            pt[h, s] = low(jnp.exp2(power))

    def attend(s):
        for h in (0, 1):
            att[h] += factor(h, s) * dot(p[h, s], head(vall, slot_rows(s), h))

    def query_grad(s):
        for h in (0, 1):
            grad = dot_nt(head(dall, mine, h), head(vall, slot_rows(s), h))
            grad = wide(p[h, s]) * ((grad - row_dot[h, :, 0:1]) * factor(h, s))
            gq[h] += dot(low(grad), head(kall, slot_rows(s), h))

    def key_grad(s):
        for h in (0, 1):
            grad_rows = head(dall, slot_rows(s), h)
            weight = pt[h, s]
            grad = dot_nt(head(vown, slice(None), h), grad_rows)
            grad = wide(weight) * (grad - stat_row(dots, s, h))
            gv[h] += dot(weight, grad_rows)
            gk[h] += dot(low(grad), head(qall, slot_rows(s), h))

    barrier = pltpu.get_barrier_semaphore()
    for half in (0, 1):
        for step in (1, -1):
            pl.semaphore_signal(
                barrier, inc=1, device_id={"tensor": block(half, step, 0)}, device_id_type=MESH
            )
    for target in (at_y(1), at_y(-1), sibling):
        pl.semaphore_signal(barrier, inc=1, device_id={"tm": target}, device_id_type=MESH)
    loads[0].wait()
    loads[1].wait()
    pl.semaphore_wait(barrier, 7)
    both(tensor_start)
    keys.start()
    both(tensor_next)
    across = lax.broadcasted_iota(jnp.int32, (F, F), 0) - lax.broadcasted_iota(jnp.int32, (F, F), 1)
    dist[...] = jnp.abs(across)
    for ref in (dacc, att, gq, gk, gv, sums):
        ref[...] = jnp.zeros_like(ref)
    tops[...] = jnp.full_like(tops, masked_score)
    for item in loads[2:]:
        item.wait()

    def keys_near():
        both(tensor_near)
        keys.near()
        queries.start()

    by_arrival(
        (keys,), softmax,
        {2: keys_near, 5: lambda: both(tensor_far), 7: lambda: forward(0)},
    )
    combine()
    totals.start()

    def queries_near():
        queries.near()
        values.start()
        totals.near()

    by_arrival(
        (queries, totals), key_side,
        {2: queries_near, 4: lambda: forward(1), 7: lambda: forward(2)},
    )
    forward(3)

    def values_near():
        values.near()

    by_arrival((values,), attend, {2: values_near})
    for index in range(4):
        finish(0, index)
    for index in range(4):
        finish(1, index)
        add_row(index)
    dall[mine, :] = low(dacc[...].T)
    grads.start()
    for h in (0, 1):
        column = jnp.sum(wide(head(dall, mine, h)) * att[h], axis=1, keepdims=True)
        row_dot[h] = jnp.broadcast_to(column, (F, HD))
        to_row(dots, h, column)
    products.start()

    def query_step(s, carry):
        query_grad(s)

        @pl.when(s == 5)
        def _():
            grads.near()
            products.near()

        return carry

    lax.fori_loop(0, 8, query_step, 0)
    keys.drain()
    values.drain()
    loads = [load(0, wk_hbm, kall), load(1, wv_hbm, vall)]
    for item in loads:
        item.start()
    gt = [p.at[0, n, 0:256] for n in range(3)]

    def to_gt(n, ref, scale):
        for h in (0, 1):
            gt[n][h * HD:(h + 1) * HD, :] = low((ref[h] * scale).T)

    to_gt(0, gq, SCALE)
    by_arrival((grads, products), key_grad, {})
    to_gt(1, gk, SCALE)
    to_gt(2, gv, 1.0)

    def drain(half):
        def one(i, carry):
            for kind in range(4):
                tensor_copy(half, 4 * i + kind, g, kind, g).wait_send()
            return carry

        lax.fori_loop(0, 5, one, 0)

    both(drain)
    for item in loads:
        item.wait()

    def target(half, d, e):
        return block(1 - half, d, e)

    def out_rows(m):
        return pl.ds(pl.multiple_of(m * 160, 32), 160)

    def out_half(m):
        return pl.ds(pl.multiple_of(3840 + m * 80, 16), 80)

    def first(m, half, step):
        return pltpu.make_async_remote_copy(
            src_ref=go.at[out_rows(m)], dst_ref=in1.at[m], send_sem=s1.at[m], recv_sem=r1.at[m],
            device_id={"tensor": target(half, step, 0)}, device_id_type=MESH,
        )

    def second(m, half, step):
        return pltpu.make_async_remote_copy(
            src_ref=go.at[out_half(m)], dst_ref=in2.at[m], send_sem=s2.at[m], recv_sem=r2.at[m],
            device_id={"tensor": target(half, 0, step)}, device_id_type=MESH,
        )

    def body(i, carry):
        t, half = i // 2, i % 2
        group, u = t // 4, t % 4
        odd = u % 2
        own_only = (group % 2) * (1 - group // 2)
        par = (odd + own_only) % 2
        e = par * (1 - u // 2) + (1 - par) * (2 + u // 2)
        near = ((group + 1) // 2) % 2
        d = near * (1 + 2 * odd) + (1 - near) * (2 - 2 * (group // 3))
        rows = pl.ds(pl.multiple_of(target(half, d, e) * 320 + half * 160, 16), 160)
        part[...] = (
            dot(wq[rows, :], gt[0][...]) + dot(kall[rows, :], gt[1][...]) + dot(vall[rows, :], gt[2][...])
        )
        step = 1 - 2 * odd

        @pl.when(group < 2)
        def _():
            m = half * 12 + t
            go[out_rows(m), :] = low(part[...])
            first(m, half, step).start()

        @pl.when(group == 2)
        def _():
            m = half * 12 + t
            first(m - 8, half, step).wait_recv()
            go[out_rows(m), :] = low(part[...] + wide(in1[m - 8]))
            first(m, half, step).start()

        @pl.when(group == 3)
        def _():
            up = half * 12 + 8 - 4 * odd + 2 * (u // 2)
            down = half * 12 + 5 + 4 * odd + 2 * (u // 2)
            first(up, half, 1).wait_recv()
            first(down, half, 1).wait_recv()
            part[...] += wide(in1[up]) + wide(in1[down])
            m = half * 6

            @pl.when(u == 0)
            def _():
                go[out_half(m), :] = low(part[0:80, :])
                second(m, half, 1).start()
                go[out_half(m + 1), :] = low(part[80:160, :])
                second(m + 1, half, -1).start()

            @pl.when(u == 1)
            def _():
                go[out_half(m + 2), :] = low(part[80:160, :])
                second(m + 2, half, 1).start()
                second(m, half, 1).wait_recv()
                go[out_half(m + 3), :] = low(part[0:80, :] + wide(in2[m]))
                second(m + 3, half, 1).start()

            @pl.when(u == 2)
            def _():
                go[out_half(m + 4), :] = low(part[0:80, :])
                second(m + 4, half, -1).start()
                second(m + 1, half, 1).wait_recv()
                go[out_half(m + 5), :] = low(part[80:160, :] + wide(in2[m + 1]))
                second(m + 5, half, -1).start()

            @pl.when(u == 3)
            def _():
                for n in (2, 3, 4, 5):
                    second(m + n, half, 1).wait_recv()
                at = pl.multiple_of(half * 160, 16)
                out_ref[pl.ds(at, 80), :] = low(part[0:80, :] + (wide(in2[m + 3]) + wide(in2[m + 4])))
                out_ref[pl.ds(at + 80, 80), :] = low(
                    part[80:160, :] + (wide(in2[m + 2]) + wide(in2[m + 5]))
                )

        return carry

    lax.fori_loop(0, 32, body, 0)

    def drain1(m, carry):
        first(m, 0, 1).wait_send()
        return carry

    def drain2(m, carry):
        second(m, 0, 1).wait_send()
        return carry

    lax.fori_loop(0, 24, drain1, 0)
    lax.fori_loop(0, 12, drain2, 0)
    for item in (queries, grads, totals, products):
        item.drain()


def per_device(queries, keys, values, grad_out, frame_map, band, w_query, w_key, w_value, w_out):
    vmem = pl.BlockSpec(memory_space=pltpu.VMEM)
    hbm = pl.BlockSpec(memory_space=pl.ANY)
    smem = pl.BlockSpec(memory_space=pltpu.SMEM)
    gathered = pltpu.VMEM((8 * F, 256), jnp.bfloat16)
    stats = pltpu.VMEM((128, F), jnp.float32)
    pairs = pltpu.VMEM((2, 8, F, F), jnp.bfloat16)
    heads = pltpu.VMEM((2, F, HD), jnp.float32)
    sems = pltpu.SemaphoreType.DMA
    return pl.pallas_call(
        kernel,
        out_shape=jax.ShapeDtypeStruct((320, F), jnp.bfloat16),
        in_specs=[smem] * 2 + [hbm] * 8,
        out_specs=vmem,
        scratch_shapes=[
            pltpu.VMEM((5120, F), jnp.bfloat16),
            pltpu.VMEM((256, 5120), jnp.bfloat16),
            gathered, gathered, gathered, gathered, gathered,
            pltpu.VMEM((F, 256), jnp.bfloat16),
            stats, stats,
            pairs, pairs,
            pltpu.VMEM((F, F), jnp.int32),
            pltpu.VMEM((256, F), jnp.float32),
            heads, heads, heads, heads, heads, heads, heads,
            pltpu.VMEM((160, F), jnp.float32),
            pltpu.VMEM((24, 160, F), jnp.bfloat16),
            pltpu.VMEM((12, 80, F), jnp.bfloat16),
            sems((7,)), sems((40,)), sems((40,)), sems((8 * ARRAYS,)), sems((8 * ARRAYS,)),
            sems((24,)), sems((24,)), sems((12,)), sems((12,)),
        ],
        compiler_params=pltpu.CompilerParams(
            collective_id=0, has_side_effects=True, vmem_limit_bytes=64 * 1024 * 1024
        ),
        cost_estimate=pl.CostEstimate(
            flops=21_000_000_000, bytes_accessed=14_000_000, transcendentals=13_000_000
        ),
    )(frame_map, band, grad_out.T, w_out, queries, keys, values, w_query, w_key, w_value)


def solution(mesh):
    placed = (
        P("tm", "tensor"),
        P("tm", "tensor"),
        P("tm", "tensor"),
        P("tm", "tensor"),
        P(),
        P(),
        P(None, "tensor"),
        P(None, "tensor"),
        P(None, "tensor"),
        P("tensor", None),
    )
    return jax.shard_map(
        per_device, mesh=mesh, in_specs=placed, out_specs=P("tensor", "tm"), check_vma=False
    )
```

time: 361 us -> 135 us (0.37)
  waiting for transfers between devices: 183 us -> 0 us
  Pallas kernels: 0 us -> 133 us
  matrix products: 116 us -> 0 us
  local copies, waits for them, and re-layouts: 25.7 us -> 1.79 us
  other arithmetic: 22.5 us -> 0 us
  between operations: 13.6 us -> 0.01 us
    pallas_call x0 -> x1, Pallas kernels: none -> 133 us  [per_device(): pl.pallas_call(kernel, out_shape=jax.ShapeDtypeStruct((320, F), jnp.bfloa...]
    dot_general x10 -> x0, matrix products: 116 us -> none  [the longest x3 29.1 us: per_device(): lax.dot_general(weight, gradient, (((1,), (1,)), ((), ())), preferred_ele...]
    reduce_scatter x1 -> x0, waiting for transfers between devices: 81.2 us -> none  [per_device(): lax.psum_scatter(total.astype(jnp.bfloat16), 'tensor', scatter_dimension=...]
    all_gather x3 -> x0, waiting for transfers between devices: 73.4 us -> none  [the longest x1 36.3 us: per_device(): lax.all_gather(grad_out, 'tensor', axis=1, tiled=True)]
    unnamed x8 -> x0, waiting for transfers between devices: 27.9 us -> none
    unnamed x10 -> x1, local copies, waits for them, and re-layouts: 23.2 us -> 1.79 us
    reduce_sum x4 -> x0, other arithmetic: 16.3 us -> none  [the longest x1 14.6 us: update(): new_total = jnp.sum(shifted, axis=2)]
    le x1 -> x0, other arithmetic: 5.4 us -> none  [pair_mask(): jnp.abs(positions[:, None] - remote_inner[None, :]) <= widths[None, :]]
  transfers between devices with their start and end apart: 6 -> 0, of which waited for: 5 -> 0; matrix products, arithmetic and copies ran while one was open for 25% -> 0% of each run, Pallas kernels for 0% -> 0%
where the time goes in v2:
time: 135 us
  Pallas kernels  133 us (99%)
  local copies, waits for them, and re-layouts  1.79 us (1%)
    pallas_call x1, Pallas kernels, per_device(): pl.pallas_call(kernel, out_shape=jax.ShapeDtypeStruct((320, F), jnp.bfloa...  133 us

profile of v2, /device:TPU:0, one launch (start us, length us, event | category | flops | bytes accessed | tf_op | source)
XLA Modules:
  0.0 134.7 jit_solution(7255096906483644045)
XLA Ops:
  0.0 132.9 %shard_map.100 = bf16[320,640]{1,0:T(8,128)(2,1)} custom-call(s32[8]{0:T(128)} %frame_map.1, s32[8,8]{1,0:T(8,128)} %band.1, bf16[320,640]{1,0:T(8,128)(2,1)} %bitcast.1, bf16[256,5120]{1,0:T(8,128)(2,1)} %wo_hbm.1, bf16[640,256]{1,0:T(8,128)(2,1)} %q_hbm.1, bf16[640,256]{1,0:T(8,128)(2,1)} %k_hbm.1, bf16[640,256]{1,0:T(8,128)(2,1)} %v_hbm.1, ...), custom_call_target="tpu_custom_call" | custom-call | flops 20999999488 | bytes 14000000 | tf_op jit(solution)/shard_map/pallas_call | solution.py:505
  132.9 1.8 %copy.12 = bf16[320,640]{1,0:T(8,128)(2,1)} copy(bf16[320,640]{1,0:T(8,128)(2,1)} %shard_map.100) | data formatting | bytes 819200

commit v3 on v2

--- a/solution.py
+++ b/solution.py
@@ -37,8 +37,8 @@
 
 def kernel(
     frame_map, band, go_hbm, wo_hbm, q_hbm, k_hbm, v_hbm, wq_hbm, wk_hbm, wv_hbm, out_ref,
-    go, wo, wq, kall, qall, vall, dall, vown, logs, dots, p, pt, dist, dacc, att, gq, gk, gv,
-    tops, sums, row_dot, part, in1, in2,
+    go, wo, kall, qall, vall, dall, vown, logs, dots, p, pt, dist, dacc, att, gq,
+    tops, sums, row_dot, in1, in2,
     load_sem, zs, zr, ys, yr, s1, r1, s2, r2,
 ):
     g = lax.axis_index("tensor")
@@ -62,7 +62,6 @@
         load(3, v_hbm, vall.at[mine]),
         load(4, v_hbm, vown),
         load(5, wo_hbm, wo),
-        load(6, wq_hbm, wq),
     ]
     for item in loads:
         item.start()
@@ -194,20 +193,20 @@
     totals, products = Gather(4, logs, 16), Gather(5, dots, 16)
 
     def by_arrival(gathers, body, events):
-        def step(n, carry):
-            ring_at = (n + 2) // 4
-            hop = (ring_at % 2) * (2 * (n % 2) - 1) + (ring_at // 2) * 2
-            other = (1 - ring_at % 2) * (n % 2) + (ring_at % 2) * (((n + 2) // 2) % 2)
-            slot = ring(y, hop) * 2 + (core + other) % 2
+        def step(i, carry):
+            n = i // 2
+            ring_at = (n + 1) // 2
+            hop = (ring_at % 2) * (2 * n - 3) + (ring_at // 2) * 2
             waits = {
-                1: lambda item: item.from_sibling(4),
-                4: lambda item: item.from_sibling(5, 6),
-                6: lambda item: item.far(),
-                7: lambda item: item.from_sibling(7),
+                0: lambda item: item.from_sibling(4),
+                2: lambda item: item.from_sibling(5),
+                4: lambda item: item.from_sibling(6),
+                5: lambda item: item.far(),
+                6: lambda item: item.from_sibling(7),
             }
             for when in range(8):
                 if when in waits or when in events:
-                    @pl.when(n == when)
+                    @pl.when(i == when)
                     def _(when=when):
                         if when in events:
                             events[when]()
@@ -215,37 +214,45 @@
                             for item in gathers:
                                 waits[when](item)
 
-            body(slot)
+            body(ring(y, hop), i % 2)
             return carry
 
         lax.fori_loop(0, 8, step, 0)
 
     lane = lax.broadcasted_iota(jnp.int32, (F, HD), 1)
 
+    def pair_rows(n):
+        return pl.ds(pl.multiple_of(n * 2 * F, 2 * F), 2 * F)
+
     def head(ref, rows, h):
-        return ref[rows, h * HD:(h + 1) * HD]
-
-    def stat_row(ref, s, h):
-        return ref[pl.ds(pl.multiple_of(s * 16 + h * 8, 8), 8), :][0:1, :]
+        return ref[rows, pl.ds(pl.multiple_of(h * HD, HD), HD)]
+
+    def stat_row(ref, n, h):
+        one = ref[pl.ds(pl.multiple_of(n * 32 + h * 8, 8), 8), :][0:1, :]
+        two = ref[pl.ds(pl.multiple_of(n * 32 + 16 + h * 8, 8), 8), :][0:1, :]
+        return jnp.concatenate([one, two], axis=1)
 
     def to_row(ref, h, column):
         rows = pl.ds(pl.multiple_of(me * 16 + h * 8, 8), 8)
         ref[rows, :] = jnp.broadcast_to(column, (F, HD)).T[0:8, :]
 
-    def factor(h, s):
-        return jnp.sum(jnp.where(lane == s, sums[h], 0.0), axis=1, keepdims=True)
-
-    def softmax(s):
-        width = band[my_frame, frame_map[s]]
-        for h in (0, 1):
-            scores = dot_nt(head(qall, mine, h), head(kall, slot_rows(s), h))
-            scores = jnp.where(dist[...] <= width, scores, masked_score)
-            top = jnp.max(scores, axis=1, keepdims=True) * POWER
-            shifted = jnp.exp2(scores * POWER - top)
-            total = jnp.sum(shifted, axis=1, keepdims=True)
-            p[h, s] = low(shifted)
-            tops[h] = jnp.where(lane == s, top, tops[h])
-            sums[h] = jnp.where(lane == s, total, sums[h])
+    def factor(h, n):
+        return jnp.sum(jnp.where(lane == n, sums[h], 0.0), axis=1, keepdims=True)
+
+    def masked(scores, first, second):
+        one = jnp.where(dist[...] <= first, scores[:, :F], masked_score)
+        two = jnp.where(dist[...] <= second, scores[:, F:], masked_score)
+        return jnp.concatenate([one, two], axis=1)
+
+    def softmax(n, h):
+        widths = [band[my_frame, frame_map[2 * n + k]] for k in (0, 1)]
+        scores = masked(dot_nt(head(qall, mine, h), head(kall, pair_rows(n), h)), *widths)
+        top = jnp.max(scores, axis=1, keepdims=True) * POWER
+        shifted = jnp.exp2(scores * POWER - top)
+        total = jnp.sum(shifted, axis=1, keepdims=True)
+        p[h, n] = low(shifted)
+        tops[h] = jnp.where(lane == n, top, tops[h])
+        sums[h] = jnp.where(lane == n, total, sums[h])
 
     def combine():
         for h in (0, 1):
@@ -255,33 +262,26 @@
             sums[h] = shares / total
             to_row(logs, h, top + jnp.log2(total))
 
-    def key_side(s):
-        width = band[frame_map[s], my_frame]
-        for h in (0, 1):
-            scores = dot_nt(head(kall, mine, h), head(qall, slot_rows(s), h))
-            power = jnp.where(
-                dist[...] <= width, scores * POWER - stat_row(logs, s, h), masked_score
-            )
-            pt[h, s] = low(jnp.exp2(power))
-
-    def attend(s):
-        for h in (0, 1):
-            att[h] += factor(h, s) * dot(p[h, s], head(vall, slot_rows(s), h))
-
-    def query_grad(s):
-        for h in (0, 1):
-            grad = dot_nt(head(dall, mine, h), head(vall, slot_rows(s), h))
-            grad = wide(p[h, s]) * ((grad - row_dot[h, :, 0:1]) * factor(h, s))
-            gq[h] += dot(low(grad), head(kall, slot_rows(s), h))
-
-    def key_grad(s):
-        for h in (0, 1):
-            grad_rows = head(dall, slot_rows(s), h)
-            weight = pt[h, s]
-            grad = dot_nt(head(vown, slice(None), h), grad_rows)
-            grad = wide(weight) * (grad - stat_row(dots, s, h))
-            gv[h] += dot(weight, grad_rows)
-            gk[h] += dot(low(grad), head(qall, slot_rows(s), h))
+    def key_side(n, h):
+        widths = [band[frame_map[2 * n + k], my_frame] for k in (0, 1)]
+        scores = dot_nt(head(kall, mine, h), head(qall, pair_rows(n), h))
+        power = masked(scores * POWER - stat_row(logs, n, h), *widths)
+        pt[h, n] = low(jnp.exp2(power))
+
+    def attend(n, h):
+        att[h] += factor(h, n) * dot(p[h, n], head(vall, pair_rows(n), h))
+
+    def query_grad(n, h):
+        grad = dot_nt(head(dall, mine, h), head(vall, pair_rows(n), h))
+        grad = low(grad - jnp.concatenate([row_dot[h]] * 10, axis=1))
+        gq[h] += factor(h, n) * dot(p[h, n] * grad, head(kall, pair_rows(n), h))
+
+    def key_grad(n, h):
+        grad_rows = head(dall, pair_rows(n), h)
+        weight = pt[h, n]
+        grad = low(dot_nt(head(vown, slice(None), h), grad_rows) - stat_row(dots, n, h))
+        gv[h] += dot(weight, grad_rows)
+        gk[h] += dot(weight * grad, head(qall, pair_rows(n), h))
 
     barrier = pltpu.get_barrier_semaphore()
     for half in (0, 1):
@@ -299,7 +299,7 @@
     both(tensor_next)
     across = lax.broadcasted_iota(jnp.int32, (F, F), 0) - lax.broadcasted_iota(jnp.int32, (F, F), 1)
     dist[...] = jnp.abs(across)
-    for ref in (dacc, att, gq, gk, gv, sums):
+    for ref in (dacc, att, gq, sums):
         ref[...] = jnp.zeros_like(ref)
     tops[...] = jnp.full_like(tops, masked_score)
     for item in loads[2:]:
@@ -344,11 +344,14 @@
         row_dot[h] = jnp.broadcast_to(column, (F, HD))
         to_row(dots, h, column)
     products.start()
-
-    def query_step(s, carry):
-        query_grad(s)
-
-        @pl.when(s == 5)
+    gk, gv = tops, att
+    for ref in (gk, gv):
+        ref[...] = jnp.zeros_like(ref)
+
+    def query_step(i, carry):
+        query_grad(i // 2, i % 2)
+
+        @pl.when(i == 5)
         def _():
             grads.near()
             products.near()
@@ -358,10 +361,10 @@
     lax.fori_loop(0, 8, query_step, 0)
     keys.drain()
     values.drain()
-    loads = [load(0, wk_hbm, kall), load(1, wv_hbm, vall)]
+    loads = [load(0, wq_hbm, kall), load(1, wk_hbm, vall)]
     for item in loads:
         item.start()
-    gt = [p.at[0, n, 0:256] for n in range(3)]
+    gt = [p.at[0, n, 0:256, 0:F] for n in range(3)]
 
     def to_gt(n, ref, scale):
         for h in (0, 1):
@@ -369,8 +372,13 @@
 
     to_gt(0, gq, SCALE)
     by_arrival((grads, products), key_grad, {})
+    queries.drain()
+    loads.append(load(2, wv_hbm, qall))
+    loads[2].start()
     to_gt(1, gk, SCALE)
     to_gt(2, gv, 1.0)
+    for item in loads:
+        item.wait()
 
     def drain(half):
         def one(i, carry):
@@ -381,115 +389,122 @@
         lax.fori_loop(0, 5, one, 0)
 
     both(drain)
-    for item in loads:
-        item.wait()
 
     def target(half, d, e):
         return block(1 - half, d, e)
 
-    def out_rows(m):
-        return pl.ds(pl.multiple_of(m * 160, 32), 160)
-
-    def out_half(m):
-        return pl.ds(pl.multiple_of(3840 + m * 80, 16), 80)
-
-    def first(m, half, step):
+    def part(half, d, e, skip=0, count=160):
+        start = target(half, d, e) * 320 + half * 160 + skip
+        return go.at[pl.ds(pl.multiple_of(start, 16), count)]
+
+    def multiply(dz):
+        def one(i, carry):
+            rows = pl.ds(pl.multiple_of(ring(z, dz) * 1280 + i * F, F), F)
+            total = dot(kall[rows, :], gt[0][...]) + dot(vall[rows, :], gt[1][...])
+            go[rows, :] = low(total + dot(qall[rows, :], gt[2][...]))
+            return carry
+
+        lax.fori_loop(0, 2, one, 0)
+
+    def first(m, half, d, e, step):
+        n = half * 12 + m
         return pltpu.make_async_remote_copy(
-            src_ref=go.at[out_rows(m)], dst_ref=in1.at[m], send_sem=s1.at[m], recv_sem=r1.at[m],
+            src_ref=part(half, d, e), dst_ref=in1.at[n], send_sem=s1.at[n], recv_sem=r1.at[n],
             device_id={"tensor": target(half, step, 0)}, device_id_type=MESH,
         )
 
-    def second(m, half, step):
+    def second(m, half, e, skip, step):
+        n = half * 6 + m
         return pltpu.make_async_remote_copy(
-            src_ref=go.at[out_half(m)], dst_ref=in2.at[m], send_sem=s2.at[m], recv_sem=r2.at[m],
+            src_ref=part(half, 0, e, skip, 80), dst_ref=in2.at[n], send_sem=s2.at[n], recv_sem=r2.at[n],
             device_id={"tensor": target(half, 0, step)}, device_id_type=MESH,
         )
 
-    def body(i, carry):
-        t, half = i // 2, i % 2
-        group, u = t // 4, t % 4
-        odd = u % 2
-        own_only = (group % 2) * (1 - group // 2)
-        par = (odd + own_only) % 2
-        e = par * (1 - u // 2) + (1 - par) * (2 + u // 2)
-        near = ((group + 1) // 2) % 2
-        d = near * (1 + 2 * odd) + (1 - near) * (2 - 2 * (group // 3))
-        rows = pl.ds(pl.multiple_of(target(half, d, e) * 320 + half * 160, 16), 160)
-        part[...] = (
-            dot(wq[rows, :], gt[0][...]) + dot(kall[rows, :], gt[1][...]) + dot(vall[rows, :], gt[2][...])
-        )
-        step = 1 - 2 * odd
-
-        @pl.when(group < 2)
-        def _():
-            m = half * 12 + t
-            go[out_rows(m), :] = low(part[...])
-            first(m, half, step).start()
-
-        @pl.when(group == 2)
-        def _():
-            m = half * 12 + t
-            first(m - 8, half, step).wait_recv()
-            go[out_rows(m), :] = low(part[...] + wide(in1[m - 8]))
-            first(m, half, step).start()
-
-        @pl.when(group == 3)
-        def _():
-            up = half * 12 + 8 - 4 * odd + 2 * (u // 2)
-            down = half * 12 + 5 + 4 * odd + 2 * (u // 2)
-            first(up, half, 1).wait_recv()
-            first(down, half, 1).wait_recv()
-            part[...] += wide(in1[up]) + wide(in1[down])
-            m = half * 6
-
-            @pl.when(u == 0)
-            def _():
-                go[out_half(m), :] = low(part[0:80, :])
-                second(m, half, 1).start()
-                go[out_half(m + 1), :] = low(part[80:160, :])
-                second(m + 1, half, -1).start()
-
-            @pl.when(u == 1)
-            def _():
-                go[out_half(m + 2), :] = low(part[80:160, :])
-                second(m + 2, half, 1).start()
-                second(m, half, 1).wait_recv()
-                go[out_half(m + 3), :] = low(part[0:80, :] + wide(in2[m]))
-                second(m + 3, half, 1).start()
-
-            @pl.when(u == 2)
-            def _():
-                go[out_half(m + 4), :] = low(part[0:80, :])
-                second(m + 4, half, -1).start()
-                second(m + 1, half, 1).wait_recv()
-                go[out_half(m + 5), :] = low(part[80:160, :] + wide(in2[m + 1]))
-                second(m + 5, half, -1).start()
-
-            @pl.when(u == 3)
-            def _():
-                for n in (2, 3, 4, 5):
-                    second(m + n, half, 1).wait_recv()
-                at = pl.multiple_of(half * 160, 16)
-                out_ref[pl.ds(at, 80), :] = low(part[0:80, :] + (wide(in2[m + 3]) + wide(in2[m + 4])))
-                out_ref[pl.ds(at + 80, 80), :] = low(
-                    part[80:160, :] + (wide(in2[m + 2]) + wide(in2[m + 5]))
-                )
-
+    far = ((0, 2, 2, 1), (1, 2, 1, -1), (2, 2, 3, 1), (3, 2, 0, -1))
+    alone = ((4, 1, 1, 1), (5, 3, 2, -1), (6, 1, 0, 1), (7, 3, 3, -1))
+    summed = ((8, 1, 2, 1), (9, 3, 1, -1), (10, 1, 3, 1), (11, 3, 0, -1))
+
+    def send(half, messages):
+        for m, d, e, step in messages:
+            first(m, half, d, e, step).start()
+
+    multiply(2)
+    send(0, far)
+    send(1, (far[0], alone[1]))
+    multiply(1)
+    send(1, (far[1],))
+    send(0, (alone[0], alone[2]))
+    send(1, (alone[0], ))
+    multiply(3)
+    send(1, (far[2], alone[3]))
+    send(0, (alone[1], alone[3]))
+    multiply(0)
+    send(1, (far[3], alone[2]))
+
+    def pass_on(m, d, e, step):
+        def one(half):
+            first(m - 8, half, d, e, step).wait_recv()
+            ref = part(half, d, e)
+            ref[...] = low(wide(ref[...]) + wide(in1[half * 12 + m - 8]))
+            first(m, half, d, e, step).start()
+
+        both(one)
+
+    for message in summed:
+        pass_on(*message)
+
+    def collect(half, e, up, down):
+        first(up, half, 0, e, 1).wait_recv()
+        first(down, half, 0, e, 1).wait_recv()
+        return wide(part(half, 0, e)[...]) + wide(in1[half * 12 + up]) + wide(in1[half * 12 + down])
+
+    def collect_far(half):
+        total = collect(half, 2, 8, 5)
+        part(half, 0, 2)[...] = low(total)
+        second(0, half, 2, 0, 1).start()
+        second(1, half, 2, 80, -1).start()
+
+    def collect_next(half):
+        total = collect(half, 1, 4, 9)
+        part(half, 0, 1)[...] = low(total)
+        second(2, half, 1, 80, 1).start()
+        total_low = total[0:80]
+        second(0, half, 1, 0, 1).wait_recv()
+        part(half, 0, 1, 0, 80)[...] = low(total_low + wide(in2[half * 6]))
+        second(3, half, 1, 0, 1).start()
+
+    def collect_last(half):
+        total = collect(half, 3, 10, 7)
+        part(half, 0, 3)[...] = low(total)
+        second(4, half, 3, 0, -1).start()
+        total_high = total[80:160]
+        second(1, half, 3, 80, -1).wait_recv()
+        part(half, 0, 3, 80, 80)[...] = low(total_high + wide(in2[half * 6 + 1]))
+        second(5, half, 3, 80, -1).start()
+
+    def collect_own(half):
+        total = collect(half, 0, 6, 11)
+        for m in (2, 3, 4, 5):
+            second(m, half, 0, 0, 1).wait_recv()
+        at = pl.multiple_of(half * 160, 16)
+        n = half * 6
+        out_ref[pl.ds(at, 80), :] = low(total[0:80] + (wide(in2[n + 3]) + wide(in2[n + 4])))
+        out_ref[pl.ds(at + 80, 80), :] = low(total[80:160] + (wide(in2[n + 2]) + wide(in2[n + 5])))
+
+    for step in (collect_far, collect_next, collect_last, collect_own):
+        both(step)
+
+    def sent1(m, carry):
+        first(m, 0, 0, 0, 1).wait_send()
         return carry
 
-    lax.fori_loop(0, 32, body, 0)
-
-    def drain1(m, carry):
-        first(m, 0, 1).wait_send()
+    def sent2(m, carry):
+        second(m, 0, 0, 0, 1).wait_send()
         return carry
 
-    def drain2(m, carry):
-        second(m, 0, 1).wait_send()
-        return carry
-
-    lax.fori_loop(0, 24, drain1, 0)
-    lax.fori_loop(0, 12, drain2, 0)
-    for item in (queries, grads, totals, products):
+    lax.fori_loop(0, 24, sent1, 0)
+    lax.fori_loop(0, 12, sent2, 0)
+    for item in (grads, totals, products):
         item.drain()
 
 
@@ -499,7 +514,7 @@
     smem = pl.BlockSpec(memory_space=pltpu.SMEM)
     gathered = pltpu.VMEM((8 * F, 256), jnp.bfloat16)
     stats = pltpu.VMEM((128, F), jnp.float32)
-    pairs = pltpu.VMEM((2, 8, F, F), jnp.bfloat16)
+    pairs = pltpu.VMEM((2, 4, F, 2 * F), jnp.bfloat16)
     heads = pltpu.VMEM((2, F, HD), jnp.float32)
     sems = pltpu.SemaphoreType.DMA
     return pl.pallas_call(
@@ -510,17 +525,16 @@
         scratch_shapes=[
             pltpu.VMEM((5120, F), jnp.bfloat16),
             pltpu.VMEM((256, 5120), jnp.bfloat16),
-            gathered, gathered, gathered, gathered, gathered,
+            gathered, gathered, gathered, gathered,
             pltpu.VMEM((F, 256), jnp.bfloat16),
             stats, stats,
             pairs, pairs,
             pltpu.VMEM((F, F), jnp.int32),
             pltpu.VMEM((256, F), jnp.float32),
-            heads, heads, heads, heads, heads, heads, heads,
-            pltpu.VMEM((160, F), jnp.float32),
+            heads, heads, heads, heads, heads,
             pltpu.VMEM((24, 160, F), jnp.bfloat16),
             pltpu.VMEM((12, 80, F), jnp.bfloat16),
-            sems((7,)), sems((40,)), sems((40,)), sems((8 * ARRAYS,)), sems((8 * ARRAYS,)),
+            sems((6,)), sems((40,)), sems((40,)), sems((8 * ARRAYS,)), sems((8 * ARRAYS,)),
             sems((24,)), sems((24,)), sems((12,)), sems((12,)),
         ],
         compiler_params=pltpu.CompilerParams(

time: 135 us -> 140 us (1.037)
  Pallas kernels: 133 us -> 138 us
    pallas_call x1, Pallas kernels: 133 us -> 138 us  [per_device(): pl.pallas_call(kernel, out_shape=jax.ShapeDtypeStruct((320, F), jnp.bfloa...]
where the time goes in v3:
time: 140 us; the launch traced here: 139 us
  Pallas kernels  138 us (99%)
  local copies, waits for them, and re-layouts  1.79 us (1%)
    pallas_call x1, Pallas kernels, per_device(): pl.pallas_call(kernel, out_shape=jax.ShapeDtypeStruct((320, F), jnp.bfloa...  138 us

profile of v3, /device:TPU:0, one launch (start us, length us, event | category | flops | bytes accessed | tf_op | source)
XLA Modules:
  0.0 139.4 jit_solution(12155824979003623436)
XLA Ops:
  0.0 137.6 %shard_map.100 = bf16[320,640]{1,0:T(8,128)(2,1)} custom-call(s32[8]{0:T(128)} %frame_map.1, s32[8,8]{1,0:T(8,128)} %band.1, bf16[320,640]{1,0:T(8,128)(2,1)} %bitcast.1, bf16[256,5120]{1,0:T(8,128)(2,1)} %wo_hbm.1, bf16[640,256]{1,0:T(8,128)(2,1)} %q_hbm.1, bf16[640,256]{1,0:T(8,128)(2,1)} %k_hbm.1, bf16[640,256]{1,0:T(8,128)(2,1)} %v_hbm.1, ...), custom_call_target="tpu_custom_call" | custom-call | flops 20999999488 | bytes 14000000 | tf_op jit(solution)/shard_map/pallas_call | solution.py:520
  137.6 1.8 %copy.12 = bf16[320,640]{1,0:T(8,128)(2,1)} copy(bf16[320,640]{1,0:T(8,128)(2,1)} %shard_map.100) | data formatting | bytes 819200

commit v4 on v3

--- a/solution.py
+++ b/solution.py
@@ -193,20 +193,20 @@
     totals, products = Gather(4, logs, 16), Gather(5, dots, 16)
 
     def by_arrival(gathers, body, events):
-        def step(i, carry):
-            n = i // 2
-            ring_at = (n + 1) // 2
-            hop = (ring_at % 2) * (2 * n - 3) + (ring_at // 2) * 2
+        def step(n, carry):
+            ring_at = (n + 2) // 4
+            hop = (ring_at % 2) * (2 * (n % 2) - 1) + (ring_at // 2) * 2
+            other = (1 - ring_at % 2) * (n % 2) + (ring_at % 2) * (((n + 2) // 2) % 2)
+            slot = ring(y, hop) * 2 + (core + other) % 2
             waits = {
-                0: lambda item: item.from_sibling(4),
-                2: lambda item: item.from_sibling(5),
-                4: lambda item: item.from_sibling(6),
-                5: lambda item: item.far(),
-                6: lambda item: item.from_sibling(7),
+                1: lambda item: item.from_sibling(4),
+                4: lambda item: item.from_sibling(5, 6),
+                6: lambda item: item.far(),
+                7: lambda item: item.from_sibling(7),
             }
             for when in range(8):
                 if when in waits or when in events:
-                    @pl.when(i == when)
+                    @pl.when(n == when)
                     def _(when=when):
                         if when in events:
                             events[when]()
@@ -214,45 +214,37 @@
                             for item in gathers:
                                 waits[when](item)
 
-            body(ring(y, hop), i % 2)
+            body(slot)
             return carry
 
         lax.fori_loop(0, 8, step, 0)
 
     lane = lax.broadcasted_iota(jnp.int32, (F, HD), 1)
 
-    def pair_rows(n):
-        return pl.ds(pl.multiple_of(n * 2 * F, 2 * F), 2 * F)
-
     def head(ref, rows, h):
-        return ref[rows, pl.ds(pl.multiple_of(h * HD, HD), HD)]
-
-    def stat_row(ref, n, h):
-        one = ref[pl.ds(pl.multiple_of(n * 32 + h * 8, 8), 8), :][0:1, :]
-        two = ref[pl.ds(pl.multiple_of(n * 32 + 16 + h * 8, 8), 8), :][0:1, :]
-        return jnp.concatenate([one, two], axis=1)
+        return ref[rows, h * HD:(h + 1) * HD]
+
+    def stat_row(ref, s, h):
+        return ref[pl.ds(pl.multiple_of(s * 16 + h * 8, 8), 8), :][0:1, :]
 
     def to_row(ref, h, column):
         rows = pl.ds(pl.multiple_of(me * 16 + h * 8, 8), 8)
         ref[rows, :] = jnp.broadcast_to(column, (F, HD)).T[0:8, :]
 
-    def factor(h, n):
-        return jnp.sum(jnp.where(lane == n, sums[h], 0.0), axis=1, keepdims=True)
-
-    def masked(scores, first, second):
-        one = jnp.where(dist[...] <= first, scores[:, :F], masked_score)
-        two = jnp.where(dist[...] <= second, scores[:, F:], masked_score)
-        return jnp.concatenate([one, two], axis=1)
-
-    def softmax(n, h):
-        widths = [band[my_frame, frame_map[2 * n + k]] for k in (0, 1)]
-        scores = masked(dot_nt(head(qall, mine, h), head(kall, pair_rows(n), h)), *widths)
-        top = jnp.max(scores, axis=1, keepdims=True) * POWER
-        shifted = jnp.exp2(scores * POWER - top)
-        total = jnp.sum(shifted, axis=1, keepdims=True)
-        p[h, n] = low(shifted)
-        tops[h] = jnp.where(lane == n, top, tops[h])
-        sums[h] = jnp.where(lane == n, total, sums[h])
+    def factor(h, s):
+        return jnp.sum(jnp.where(lane == s, sums[h], 0.0), axis=1, keepdims=True)
+
+    def softmax(s):
+        width = band[my_frame, frame_map[s]]
+        for h in (0, 1):
+            scores = dot_nt(head(qall, mine, h), head(kall, slot_rows(s), h))
+            scores = jnp.where(dist[...] <= width, scores, masked_score)
+            top = jnp.max(scores, axis=1, keepdims=True) * POWER
+            shifted = jnp.exp2(scores * POWER - top)
+            total = jnp.sum(shifted, axis=1, keepdims=True)
+            p[h, s] = low(shifted)
+            tops[h] = jnp.where(lane == s, top, tops[h])
+            sums[h] = jnp.where(lane == s, total, sums[h])
 
     def combine():
         for h in (0, 1):
@@ -262,26 +254,33 @@
             sums[h] = shares / total
             to_row(logs, h, top + jnp.log2(total))
 
-    def key_side(n, h):
-        widths = [band[frame_map[2 * n + k], my_frame] for k in (0, 1)]
-        scores = dot_nt(head(kall, mine, h), head(qall, pair_rows(n), h))
-        power = masked(scores * POWER - stat_row(logs, n, h), *widths)
-        pt[h, n] = low(jnp.exp2(power))
-
-    def attend(n, h):
-        att[h] += factor(h, n) * dot(p[h, n], head(vall, pair_rows(n), h))
-
-    def query_grad(n, h):
-        grad = dot_nt(head(dall, mine, h), head(vall, pair_rows(n), h))
-        grad = low(grad - jnp.concatenate([row_dot[h]] * 10, axis=1))
-        gq[h] += factor(h, n) * dot(p[h, n] * grad, head(kall, pair_rows(n), h))
-
-    def key_grad(n, h):
-        grad_rows = head(dall, pair_rows(n), h)
-        weight = pt[h, n]
-        grad = low(dot_nt(head(vown, slice(None), h), grad_rows) - stat_row(dots, n, h))
-        gv[h] += dot(weight, grad_rows)
-        gk[h] += dot(weight * grad, head(qall, pair_rows(n), h))
+    def key_side(s):
+        width = band[frame_map[s], my_frame]
+        for h in (0, 1):
+            scores = dot_nt(head(kall, mine, h), head(qall, slot_rows(s), h))
+            power = jnp.where(
+                dist[...] <= width, scores * POWER - stat_row(logs, s, h), masked_score
+            )
+            pt[h, s] = low(jnp.exp2(power))
+
+    def attend(s):
+        for h in (0, 1):
+            att[h] += factor(h, s) * dot(p[h, s], head(vall, slot_rows(s), h))
+
+    def query_grad(s):
+        for h in (0, 1):
+            grad = dot_nt(head(dall, mine, h), head(vall, slot_rows(s), h))
+            grad = wide(p[h, s]) * ((grad - row_dot[h, :, 0:1]) * factor(h, s))
+            gq[h] += dot(low(grad), head(kall, slot_rows(s), h))
+
+    def key_grad(s):
+        for h in (0, 1):
+            grad_rows = head(dall, slot_rows(s), h)
+            weight = pt[h, s]
+            grad = dot_nt(head(vown, slice(None), h), grad_rows)
+            grad = wide(weight) * (grad - stat_row(dots, s, h))
+            gv[h] += dot(weight, grad_rows)
+            gk[h] += dot(low(grad), head(qall, slot_rows(s), h))
 
     barrier = pltpu.get_barrier_semaphore()
     for half in (0, 1):
@@ -348,10 +347,10 @@
     for ref in (gk, gv):
         ref[...] = jnp.zeros_like(ref)
 
-    def query_step(i, carry):
-        query_grad(i // 2, i % 2)
-
-        @pl.when(i == 5)
+    def query_step(s, carry):
+        query_grad(s)
+
+        @pl.when(s == 5)
         def _():
             grads.near()
             products.near()
@@ -364,7 +363,7 @@
     loads = [load(0, wq_hbm, kall), load(1, wk_hbm, vall)]
     for item in loads:
         item.start()
-    gt = [p.at[0, n, 0:256, 0:F] for n in range(3)]
+    gt = [p.at[0, n, 0:256] for n in range(3)]
 
     def to_gt(n, ref, scale):
         for h in (0, 1):
@@ -514,7 +513,7 @@
     smem = pl.BlockSpec(memory_space=pltpu.SMEM)
     gathered = pltpu.VMEM((8 * F, 256), jnp.bfloat16)
     stats = pltpu.VMEM((128, F), jnp.float32)
-    pairs = pltpu.VMEM((2, 4, F, 2 * F), jnp.bfloat16)
+    pairs = pltpu.VMEM((2, 8, F, F), jnp.bfloat16)
     heads = pltpu.VMEM((2, F, HD), jnp.float32)
     sems = pltpu.SemaphoreType.DMA
     return pl.pallas_call(

time: 140 us -> 137 us (0.979)
  Pallas kernels: 138 us -> 135 us
    pallas_call x1, Pallas kernels: 138 us -> 135 us  [per_device(): pl.pallas_call(kernel, out_shape=jax.ShapeDtypeStruct((320, F), jnp.bfloa...]
where the time goes in v4:
time: 137 us
  Pallas kernels  135 us (99%)
  local copies, waits for them, and re-layouts  1.79 us (1%)
    pallas_call x1, Pallas kernels, per_device(): pl.pallas_call(kernel, out_shape=jax.ShapeDtypeStruct((320, F), jnp.bfloa...  135 us

profile of v4, /device:TPU:0, one launch (start us, length us, event | category | flops | bytes accessed | tf_op | source)
XLA Modules:
  0.0 136.9 jit_solution(11381367328921350718)
XLA Ops:
  0.0 135.1 %shard_map.100 = bf16[320,640]{1,0:T(8,128)(2,1)} custom-call(s32[8]{0:T(128)} %frame_map.1, s32[8,8]{1,0:T(8,128)} %band.1, bf16[320,640]{1,0:T(8,128)(2,1)} %bitcast.1, bf16[256,5120]{1,0:T(8,128)(2,1)} %wo_hbm.1, bf16[640,256]{1,0:T(8,128)(2,1)} %q_hbm.1, bf16[640,256]{1,0:T(8,128)(2,1)} %k_hbm.1, bf16[640,256]{1,0:T(8,128)(2,1)} %v_hbm.1, ...), custom_call_target="tpu_custom_call" | custom-call | flops 20999999488 | bytes 14000000 | tf_op jit(solution)/shard_map/pallas_call | solution.py:519
  135.2 1.8 %copy.12 = bf16[320,640]{1,0:T(8,128)(2,1)} copy(bf16[320,640]{1,0:T(8,128)(2,1)} %shard_map.100) | data formatting | bytes 819200

commit v5 on v4

v5 whole, which is shorter than its diff:
```python
import jax
import jax.numpy as jnp
from jax import lax
from jax.experimental import pallas as pl
from jax.experimental.pallas import tpu as pltpu
from jax.sharding import PartitionSpec as P

HD = 128
F = 640
SCALE = HD ** -0.5
POWER = SCALE * 1.4426950408889634
ARRAYS = 6
CHUNKS = ((0, 384), (384, 256))
MESH = pl.DeviceIdType.MESH
NT = (((1,), (1,)), ((), ()))
masked_score = -1e30


def dot(a, b):
    return jnp.dot(a, b, preferred_element_type=jnp.float32)


def dot_nt(a, b):
    return lax.dot_general(a, b, NT, preferred_element_type=jnp.float32)


def ring(position, step):
    return lax.rem(position + step + 4, 4)


def low(value):
    return value.astype(jnp.bfloat16)


def wide(value):
    return value.astype(jnp.float32)


def kernel(
    frame_map, band, go_hbm, wo_hbm, q_hbm, k_hbm, v_hbm, wq_hbm, wk_hbm, wv_hbm, out_ref,
    go, wo, wq, wk, wv, qall, dall, kown, vown, ktr, vtr, stage, stats, shares, dots0, dots1, pt, dist,
    dacc, att, gk, gv, abuf, asib, aopp, afin, qbuf0, qsib0, qopp0, qfin0, qbuf1, qsib1, qopp1, qfin1, gt, in1, in2,
    load_sem, zs, zr, ys, yr, ts, tr, s1, r1, s2, r2,
):
    g = lax.axis_index("tensor")
    z, x = g // 4, g % 4
    me = lax.axis_index("tm")
    y, core = me // 2, me % 2
    my_frame = frame_map[me]

    def slot_rows(s):
        return pl.ds(pl.multiple_of(s * F, F), F)

    mine = slot_rows(me)

    def load(n, src, dst):
        return pltpu.make_async_copy(src, dst, load_sem.at[n])

    loads = [
        load(0, go_hbm, go.at[pl.ds(pl.multiple_of(g * 320, 320), 320)]),
        load(1, q_hbm, qall.at[mine]),
        load(2, k_hbm, kown),
        load(3, v_hbm, vown),
        load(4, wo_hbm, wo),
        load(5, wq_hbm, wq),
        load(6, wk_hbm, wk),
        load(7, wv_hbm, wv),
    ]
    for item in loads:
        item.start()

    def block(half, d, e):
        zz = ring(z, d * half + e * (1 - half))
        xx = ring(x, d * (1 - half) + e * half)
        return zz * 4 + xx

    def tokens(c):
        return slice(CHUNKS[c][0], sum(CHUNKS[c]))

    def tensor_copy(c, half, m, j, kind, target):
        start = j * 320 + half * 160 + (80 if kind == 3 else 0)
        ref = go.at[pl.ds(pl.multiple_of(start, 16), 160 if kind < 2 else 80), tokens(c)]
        n = c * 40 + half * 20 + m
        return pltpu.make_async_remote_copy(
            src_ref=ref, dst_ref=ref, send_sem=zs.at[n], recv_sem=zr.at[n],
            device_id={"tensor": target}, device_id_type=MESH,
        )

    def both(step):
        def one(half, carry):
            step(half)
            return carry

        lax.fori_loop(0, 2, one, 0)

    def spread(c, half, index, d):
        j = block(half, d, 0)
        m = 4 + 4 * index
        tensor_copy(c, half, m, j, 0, block(half, 0, 1)).start()
        tensor_copy(c, half, m + 1, j, 1, block(half, 0, -1)).start()

    def tensor_start(c):
        def step(half):
            tensor_copy(c, half, 0, g, 0, block(half, 1, 0)).start()
            tensor_copy(c, half, 1, g, 1, block(half, -1, 0)).start()

        both(step)

    def tensor_next(c):
        both(lambda half: spread(c, half, 0, 0))

    def tensor_near(c):
        def step(half):
            j = block(half, -1, 0)
            tensor_copy(c, half, 0, j, 0, g).wait_recv()
            tensor_copy(c, half, 2, j, 2, block(half, 1, 0)).start()
            spread(c, half, 1, -1)
            j = block(half, 1, 0)
            tensor_copy(c, half, 1, j, 1, g).wait_recv()
            tensor_copy(c, half, 3, j, 3, block(half, -1, 0)).start()
            spread(c, half, 2, 1)

        both(step)

    def tensor_far(c):
        def step(half):
            j = block(half, 2, 0)
            tensor_copy(c, half, 2, j, 2, g).wait_recv()
            tensor_copy(c, half, 3, j, 3, g).wait_recv()
            spread(c, half, 3, 2)

        both(step)

    offsets = (0, -1, 1, 2)

    def forward(c, index):
        def step(half):
            m, d = 4 + 4 * index, offsets[index]
            j = block(half, d, -1)
            tensor_copy(c, half, m, j, 0, g).wait_recv()
            tensor_copy(c, half, m + 2, j, 2, block(half, 0, 1)).start()
            j = block(half, d, 1)
            tensor_copy(c, half, m + 1, j, 1, g).wait_recv()
            tensor_copy(c, half, m + 3, j, 3, block(half, 0, -1)).start()

        both(step)

    def finish(c, half, index):
        m, d = 4 + 4 * index, offsets[index]
        j = block(half, d, 2)
        tensor_copy(c, half, m + 2, j, 2, g).wait_recv()
        tensor_copy(c, half, m + 3, j, 3, g).wait_recv()

    def add_row(c, index):
        cols = pl.ds(pl.multiple_of(ring(z, offsets[index]) * 1280, 1280), 1280)
        dacc[:, tokens(c)] += dot(wo[:, cols], go[cols, tokens(c)])

    sibling = y * 2 + 1 - core

    def at_y(step):
        return ring(y, step) * 2 + core

    class Gather:
        def __init__(self, array, ref, rows, stride=None, offset=0):
            self.array, self.ref, self.rows = array, ref, rows
            self.stride, self.offset = stride or rows, offset

        def copy(self, m, slot, target):
            start, count = slot * self.stride + self.offset, self.rows
            if m in (2, 3):
                count = self.rows // 2
                start = start + (m - 2) * count
            ref = self.ref.at[pl.ds(pl.multiple_of(start, 16 if count % 16 == 0 else 8), count)]
            n = self.array * 8 + m
            return pltpu.make_async_remote_copy(
                src_ref=ref, dst_ref=ref, send_sem=ys.at[n], recv_sem=yr.at[n],
                device_id={"tm": target}, device_id_type=MESH,
            )

        def start(self):
            self.copy(0, me, at_y(1)).start()
            self.copy(1, me, at_y(-1)).start()
            self.copy(4, me, sibling).start()

        def near(self):
            self.copy(0, at_y(-1), me).wait_recv()
            self.copy(2, at_y(-1), at_y(1)).start()
            self.copy(5, at_y(-1), sibling).start()
            self.copy(1, at_y(1), me).wait_recv()
            self.copy(3, at_y(1), at_y(-1)).start()
            self.copy(6, at_y(1), sibling).start()

        def far(self):
            self.copy(2, at_y(2), me).wait_recv()
            self.copy(3, at_y(2), me).wait_recv()
            self.copy(7, at_y(2), sibling).start()

        def from_sibling(self, *messages):
            for m in messages:
                slot = ring(y, (0, -1, 1, 2)[m - 4]) * 2 + 1 - core
                self.copy(m, slot, me).wait_recv()

        def drain(self):
            for m in range(8):
                self.copy(m, me, me).wait_send()

    queries, blocks = Gather(0, qall, F), Gather(1, stats, 32)
    grads = [Gather(2 + c, dall, CHUNKS[c][1], F, CHUNKS[c][0]) for c in (0, 1)]
    dots = (dots0, dots1)
    products = [Gather(4 + c, dots[c], 16) for c in (0, 1)]

    class Scatter:
        def __init__(self, array, buf, from_core, far, last):
            self.array, self.buf, self.from_core, self.far, self.last = array, buf, from_core, far, last

        def rows(self, k, other, skip=0, count=256):
            slot = ring(y, (2, 1, -1, 0)[k]) * 2 + (core + other) % 2
            return pl.ds(pl.multiple_of(slot * 256 + skip, 128), count)

        def copy(self, m, src, dst, target):
            n = self.array * 10 + m
            return pltpu.make_async_remote_copy(
                src_ref=self.buf.at[src], dst_ref=dst, send_sem=ts.at[n], recv_sem=tr.at[n],
                device_id={"tm": target}, device_id_type=MESH,
            )

        def core_copy(self, k):
            return self.copy(k, self.rows(k, 1), self.from_core.at[k], sibling)

        def half_copy(self, m):
            k = {4: 0, 5: 0, 6: 1, 7: 1, 8: 2, 9: 2}[m]
            skip = {4: 0, 5: 128, 6: 128, 7: 0, 8: 0, 9: 128}[m]
            up = m in (4, 6, 7)
            if m < 6:
                dst = self.far.at[m - 4]
            else:
                dst = self.last.at[0 if up else 1, skip:skip + 128]
            return self.copy(m, self.rows(k, 0, skip, 128), dst, at_y(1 if up else -1))

        def merge(self, k):
            self.core_copy(k).wait_recv()
            rows = self.rows(k, 0)
            total = wide(self.buf[rows, :]) + wide(self.from_core[k])
            if k == 3:
                for m in (6, 7, 8, 9):
                    self.half_copy(m).wait_recv()
                return total + (wide(self.last[0]) + wide(self.last[1]))
            self.buf[rows, :] = low(total)
            if k == 0:
                self.half_copy(4).start()
                self.half_copy(5).start()
                return None
            ready, later, wait, skip = ((6, 7, 4, 0), (8, 9, 5, 128))[k - 1]
            self.half_copy(ready).start()
            self.half_copy(wait).wait_recv()
            self.buf[self.rows(k, 0, skip, 128), :] = low(total[skip:skip + 128] + wide(self.far[wait - 4]))
            self.half_copy(later).start()
            return None

        def drain(self):
            for k in range(4):
                self.core_copy(k).wait_send()
            for m in range(4, 10):
                self.half_copy(m).wait_send()

    attended = Scatter(0, abuf, asib, aopp, afin)
    query_grads = (Scatter(1, qbuf0, qsib0, qopp0, qfin0), Scatter(2, qbuf1, qsib1, qopp1, qfin1))
    qbuf = (qbuf0, qbuf1)

    def by_arrival(body, before, after):
        def step(n, carry):
            def run(events):
                for when in events:
                    @pl.when(n == when)
                    def _(when=when):
                        events[when]()

            run(before)
            body(ring(y, (4 - n // 2) % 4) * 2 + (core + n % 2) % 2)
            run(after)
            return carry

        lax.fori_loop(0, 8, step, 0)

    def slot_waits(gathers, events):
        def at(n):
            def run():
                if n in events:
                    events[n]()
                for item in gathers:
                    if n == 4:
                        item.far()
                    if n in (1, 3, 5, 7):
                        item.from_sibling({1: 4, 3: 5, 5: 7, 7: 6}[n])

            return run

        return {n: at(n) for n in range(1, 8)}

    def rows_of(h):
        return slice(h * HD, (h + 1) * HD)

    def head(ref, rows, h):
        return ref[rows, rows_of(h)]

    def stat_row(ref, s, h):
        return ref[pl.ds(pl.multiple_of(s * 16 + h * 8, 8), 8), :][0:1, :]

    def slot_lanes(s, h):
        return pl.ds(pl.multiple_of(s * 256 + h * HD, HD), HD)

    def scores_side(s):
        width = band[frame_map[s], my_frame]
        rows = []
        for h in (0, 1):
            scores = dot_nt(kown[:, rows_of(h)], head(qall, slot_rows(s), h))
            scores = jnp.where(dist[...] <= width, scores, masked_score)
            top = jnp.max(scores, axis=0, keepdims=True) * POWER
            shifted = jnp.exp2(scores * POWER - top)
            weight = low(shifted)
            pt[h, s] = weight
            abuf[slot_lanes(s, h), :] = low(dot(vtr[rows_of(h), :], weight))
            rows.append((top, jnp.sum(shifted, axis=0, keepdims=True)))
        (top0, sum0), (top1, sum1) = rows
        stage[pl.ds(pl.multiple_of(s * 8, 8), 8), :] = jnp.concatenate(
            [top0, top1, sum0, sum1, top0, top1, sum0, sum1], axis=0
        )

    def share_blocks():
        base = me * 32
        for k in (0, 1):
            for first_row, skip in ((0, 0), (16, 2)):
                tile = [stage[s * 8 + skip:s * 8 + skip + 2, :] for s in range(4 * k, 4 * k + 4)]
                at = pl.ds(pl.multiple_of(base + first_row + 8 * k, 8), 8)
                stats[at, :] = jnp.concatenate(tile, axis=0)

    def combine():
        tops = [stats[s * 32:s * 32 + 16, :] for s in range(8)]
        top = tops[0]
        for one in tops[1:]:
            top = jnp.maximum(top, one)
        total = jnp.zeros_like(top)
        for s in range(8):
            total += stats[s * 32 + 16:s * 32 + 32, :] * jnp.exp2(tops[s] - top)
        own = stats[pl.ds(pl.multiple_of(me * 32, 16), 16), :]
        share = jnp.exp2(own - (top + jnp.log2(total)))
        for n in range(16):
            shares[n * 8:(n + 1) * 8, :] = jnp.broadcast_to(share[n:n + 1, :], (8, F))

    def scale_attended(s):
        for h in (0, 1):
            rows = slot_lanes(s, h)
            abuf[rows, :] = low(wide(abuf[rows, :]) * stat_row(shares, s, h))

    def scale_probs(s):
        for h in (0, 1):
            pt[h, s] = low(wide(pt[h, s]) * stat_row(shares, s, h))

    def gradients(c):
        at, count = CHUNKS[c]

        def step(s):
            rows = pl.ds(pl.multiple_of(s * F + at, 128), count)
            for h in (0, 1):
                grad_rows = head(dall, rows, h)
                weight = pt[h, s, :, tokens(c)]
                grad = low(dot_nt(vown[:, rows_of(h)], grad_rows) - stat_row(dots[c], s, h))
                grad = weight * grad
                gv[h] += dot(weight, grad_rows)
                gk[h] += dot(grad, head(qall, rows, h))
                qbuf[c][slot_lanes(s, h), :] = low(dot(ktr[rows_of(h), :], grad) * SCALE)

        return step

    barrier = pltpu.get_barrier_semaphore()
    for half in (0, 1):
        for step in (1, -1):
            pl.semaphore_signal(
                barrier, inc=1, device_id={"tensor": block(half, step, 0)}, device_id_type=MESH
            )
    for target in (at_y(1), at_y(-1), sibling):
        pl.semaphore_signal(barrier, inc=1, device_id={"tm": target}, device_id_type=MESH)
    loads[0].wait()
    loads[1].wait()
    pl.semaphore_wait(barrier, 7)
    tensor_start(0)
    queries.start()
    tensor_next(0)
    across = lax.broadcasted_iota(jnp.int32, (F, F), 0) - lax.broadcasted_iota(jnp.int32, (F, F), 1)
    dist[...] = jnp.abs(across)
    for ref in (dacc, gk, gv):
        ref[...] = jnp.zeros_like(ref)
    for item in loads[2:]:
        item.wait()
    ktr[...] = low(wide(kown[...]).T)
    vtr[...] = low(wide(vown[...]).T)

    def queries_near():
        tensor_near(0)
        queries.near()

    by_arrival(
        scores_side,
        slot_waits((queries,), {
            2: queries_near,
            4: lambda: tensor_far(0),
            5: lambda: forward(0, 0),
            6: lambda: forward(0, 1),
            7: lambda: forward(0, 2),
        }),
        {},
    )
    share_blocks()
    blocks.start()
    forward(0, 3)
    tensor_start(1)
    blocks.near()
    blocks.from_sibling(4)
    blocks.far()
    tensor_next(1)
    blocks.from_sibling(5, 6, 7)
    combine()

    def eight(step):
        def one(s, carry):
            step(s)
            return carry

        lax.fori_loop(0, 8, one, 0)

    eight(scale_attended)
    for k in range(4):
        attended.core_copy(k).start()
    tensor_near(1)

    def probs_step(s):
        scale_probs(s)
        events = {
            1: lambda: attended.merge(0),
            3: lambda: tensor_far(1),
            6: lambda: attended.merge(1),
            7: lambda: attended.merge(2),
        }
        for when in events:
            @pl.when(s == when)
            def _(when=when):
                events[when]()

    eight(probs_step)

    def form_output_grad(c):
        at, count = CHUNKS[c]
        for index in range(4):
            finish(c, 0, index)
        for index in range(4):
            finish(c, 1, index)
            add_row(c, index)
        rows = pl.ds(pl.multiple_of(me * F + at, 128), count)
        dall[rows, :] = low(dacc[:, tokens(c)].T)
        grads[c].start()

    def form_row_dots(c):
        for h in (0, 1):
            own = wide(low(dacc[rows_of(h), tokens(c)])) * att[rows_of(h), tokens(c)]
            row = jnp.sum(own, axis=0, keepdims=True)
            at = pl.ds(pl.multiple_of(me * 16 + h * 8, 8), 8)
            dots[c][at, :] = jnp.broadcast_to(row, (8, CHUNKS[c][1]))
        products[c].start()

    def run_gradients(c, events):
        def near():
            grads[c].near()
            products[c].near()

        scatter = query_grads[c]
        by_arrival(
            gradients(c),
            slot_waits((grads[c], products[c]), {2: near, **events}),
            {
                1: lambda: scatter.core_copy(3).start(),
                3: lambda: scatter.core_copy(2).start(),
                5: lambda: scatter.core_copy(0).start(),
                6: lambda: scatter.merge(0),
                7: lambda: scatter.core_copy(1).start(),
            },
        )

    form_output_grad(0)
    forward(1, 0)
    att[...] = attended.merge(3)
    form_row_dots(0)
    forward(1, 1)
    run_gradients(0, {3: lambda: forward(1, 2), 5: lambda: forward(1, 3)})
    query_grads[0].merge(2)
    query_grads[0].merge(1)
    form_output_grad(1)
    form_row_dots(1)
    gt[0, :, tokens(0)] = low(query_grads[0].merge(3))
    run_gradients(1, {})

    def to_gt(n, ref, scale):
        for h in (0, 1):
            gt[n, rows_of(h), :] = low((ref[h] * scale).T)

    query_grads[1].merge(2)
    to_gt(1, gk, SCALE)
    query_grads[1].merge(1)
    to_gt(2, gv, 1.0)
    gt[0, :, tokens(1)] = low(query_grads[1].merge(3))

    def drain(half):
        def one(i, carry):
            for kind in range(4):
                for c in (0, 1):
                    tensor_copy(c, half, 4 * i + kind, g, kind, g).wait_send()
            return carry

        lax.fori_loop(0, 5, one, 0)

    both(drain)

    def target(half, d, e):
        return block(1 - half, d, e)

    def part(half, d, e, skip=0, count=160):
        start = target(half, d, e) * 320 + half * 160 + skip
        return go.at[pl.ds(pl.multiple_of(start, 16), count)]

    def multiply(dz):
        def one(i, carry):
            rows = pl.ds(pl.multiple_of(ring(z, dz) * 1280 + i * F, F), F)
            total = dot(wq[rows, :], gt[0]) + dot(wk[rows, :], gt[1])
            go[rows, :] = low(total + dot(wv[rows, :], gt[2]))
            return carry

        lax.fori_loop(0, 2, one, 0)

    def first(m, half, d, e, step):
        n = half * 12 + m
        return pltpu.make_async_remote_copy(
            src_ref=part(half, d, e), dst_ref=in1.at[n], send_sem=s1.at[n], recv_sem=r1.at[n],
            device_id={"tensor": target(half, step, 0)}, device_id_type=MESH,
        )

    def second(m, half, e, skip, step):
        n = half * 6 + m
        return pltpu.make_async_remote_copy(
            src_ref=part(half, 0, e, skip, 80), dst_ref=in2.at[n], send_sem=s2.at[n], recv_sem=r2.at[n],
            device_id={"tensor": target(half, 0, step)}, device_id_type=MESH,
        )

    far = ((0, 2, 2, 1), (1, 2, 1, -1), (2, 2, 3, 1), (3, 2, 0, -1))
    alone = ((4, 1, 1, 1), (5, 3, 2, -1), (6, 1, 0, 1), (7, 3, 3, -1))
    summed = ((8, 1, 2, 1), (9, 3, 1, -1), (10, 1, 3, 1), (11, 3, 0, -1))

    def send(half, messages):
        for m, d, e, step in messages:
            first(m, half, d, e, step).start()

    multiply(2)
    send(0, far)
    send(1, (far[0], alone[1]))
    multiply(1)
    send(1, (far[1],))
    send(0, (alone[0], alone[2]))
    send(1, (alone[0], ))
    multiply(3)
    send(1, (far[2], alone[3]))
    send(0, (alone[1], alone[3]))
    multiply(0)
    send(1, (far[3], alone[2]))

    def pass_on(m, d, e, step):
        def one(half):
            first(m - 8, half, d, e, step).wait_recv()
            ref = part(half, d, e)
            ref[...] = low(wide(ref[...]) + wide(in1[half * 12 + m - 8]))
            first(m, half, d, e, step).start()

        both(one)

    for message in summed:
        pass_on(*message)

    def collect(half, e, up, down):
        first(up, half, 0, e, 1).wait_recv()
        first(down, half, 0, e, 1).wait_recv()
        return wide(part(half, 0, e)[...]) + wide(in1[half * 12 + up]) + wide(in1[half * 12 + down])

    def collect_far(half):
        total = collect(half, 2, 8, 5)
        part(half, 0, 2)[...] = low(total)
        second(0, half, 2, 0, 1).start()
        second(1, half, 2, 80, -1).start()

    def collect_next(half):
        total = collect(half, 1, 4, 9)
        part(half, 0, 1)[...] = low(total)
        second(2, half, 1, 80, 1).start()
        total_low = total[0:80]
        second(0, half, 1, 0, 1).wait_recv()
        part(half, 0, 1, 0, 80)[...] = low(total_low + wide(in2[half * 6]))
        second(3, half, 1, 0, 1).start()

    def collect_last(half):
        total = collect(half, 3, 10, 7)
        part(half, 0, 3)[...] = low(total)
        second(4, half, 3, 0, -1).start()
        total_high = total[80:160]
        second(1, half, 3, 80, -1).wait_recv()
        part(half, 0, 3, 80, 80)[...] = low(total_high + wide(in2[half * 6 + 1]))
        second(5, half, 3, 80, -1).start()

    def collect_own(half):
        total = collect(half, 0, 6, 11)
        for m in (2, 3, 4, 5):
            second(m, half, 0, 0, 1).wait_recv()
        at = pl.multiple_of(half * 160, 16)
        n = half * 6
        out_ref[pl.ds(at, 80), :] = low(total[0:80] + (wide(in2[n + 3]) + wide(in2[n + 4])))
        out_ref[pl.ds(at + 80, 80), :] = low(total[80:160] + (wide(in2[n + 2]) + wide(in2[n + 5])))

    for step in (collect_far, collect_next, collect_last, collect_own):
        both(step)

    def sent1(m, carry):
        first(m, 0, 0, 0, 1).wait_send()
        return carry

    def sent2(m, carry):
        second(m, 0, 0, 0, 1).wait_send()
        return carry

    lax.fori_loop(0, 24, sent1, 0)
    lax.fori_loop(0, 12, sent2, 0)
    for item in (queries, blocks, *grads, *products, attended, *query_grads):
        item.drain()


def per_device(queries, keys, values, grad_out, frame_map, band, w_query, w_key, w_value, w_out):
    vmem = pl.BlockSpec(memory_space=pltpu.VMEM)
    hbm = pl.BlockSpec(memory_space=pl.ANY)
    smem = pl.BlockSpec(memory_space=pltpu.SMEM)
    bf16, f32 = jnp.bfloat16, jnp.float32
    gathered = pltpu.VMEM((8 * F, 256), bf16)
    weight = pltpu.VMEM((5120, 256), bf16)
    own = pltpu.VMEM((F, 256), bf16)
    turned = pltpu.VMEM((256, F), bf16)
    heads = pltpu.VMEM((2, F, HD), f32)
    scattered = [
        pltpu.VMEM((*rows, width), bf16)
        for width in (F, CHUNKS[0][1], CHUNKS[1][1])
        for rows in ((8 * 256,), (4, 256), (2, 128), (2, 256))
    ]
    sems = pltpu.SemaphoreType.DMA
    return pl.pallas_call(
        kernel,
        out_shape=jax.ShapeDtypeStruct((320, F), jnp.bfloat16),
        in_specs=[smem] * 2 + [hbm] * 8,
        out_specs=vmem,
        scratch_shapes=[
            pltpu.VMEM((5120, F), jnp.bfloat16),
            pltpu.VMEM((256, 5120), bf16),
            weight, weight, weight, gathered, gathered, own, own, turned, turned,
            pltpu.VMEM((64, F), f32),
            pltpu.VMEM((256, F), f32),
            pltpu.VMEM((128, F), f32),
            pltpu.VMEM((128, CHUNKS[0][1]), f32),
            pltpu.VMEM((128, CHUNKS[1][1]), f32),
            pltpu.VMEM((2, 8, F, F), bf16),
            pltpu.VMEM((F, F), jnp.int32),
            pltpu.VMEM((256, F), f32),
            pltpu.VMEM((256, F), f32),
            heads, heads, *scattered,
            pltpu.VMEM((3, 256, F), bf16),
            pltpu.VMEM((24, 160, F), jnp.bfloat16),
            pltpu.VMEM((12, 80, F), jnp.bfloat16),
            sems((8,)), sems((80,)), sems((80,)), sems((8 * ARRAYS,)), sems((8 * ARRAYS,)),
            sems((30,)), sems((30,)),
            sems((24,)), sems((24,)), sems((12,)), sems((12,)),
        ],
        compiler_params=pltpu.CompilerParams(
            collective_id=0, has_side_effects=True, vmem_limit_bytes=64 * 1024 * 1024
        ),
        cost_estimate=pl.CostEstimate(
            flops=21_000_000_000, bytes_accessed=14_000_000, transcendentals=13_000_000
        ),
    )(frame_map, band, grad_out.T, w_out, queries, keys, values, w_query, w_key, w_value)


def solution(mesh):
    placed = (
        P("tm", "tensor"),
        P("tm", "tensor"),
        P("tm", "tensor"),
        P("tm", "tensor"),
        P(),
        P(),
        P(None, "tensor"),
        P(None, "tensor"),
        P(None, "tensor"),
        P("tensor", None),
    )
    return jax.shard_map(
        per_device, mesh=mesh, in_specs=placed, out_specs=P("tensor", "tm"), check_vma=False
    )
```

time: 137 us -> 146 us (1.066)
  Pallas kernels: 135 us -> 144 us
    pallas_call x1, Pallas kernels: 135 us -> 144 us  [per_device(): pl.pallas_call(kernel, out_shape=jax.ShapeDtypeStruct((320, F), jnp.bfloa...]
where the time goes in v5:
time: 146 us
  Pallas kernels  144 us (99%)
  local copies, waits for them, and re-layouts  1.79 us (1%)
    pallas_call x1, Pallas kernels, per_device(): pl.pallas_call(kernel, out_shape=jax.ShapeDtypeStruct((320, F), jnp.bfloa...  144 us

profile of v5, /device:TPU:0, one launch (start us, length us, event | category | flops | bytes accessed | tf_op | source)
XLA Modules:
  0.0 145.9 jit_solution(5409929431503885067)
XLA Ops:
  0.0 144.1 %shard_map.100 = bf16[320,640]{1,0:T(8,128)(2,1)} custom-call(s32[8]{0:T(128)} %frame_map.1, s32[8,8]{1,0:T(8,128)} %band.1, bf16[320,640]{1,0:T(8,128)(2,1)} %bitcast.1, bf16[256,5120]{1,0:T(8,128)(2,1)} %wo_hbm.1, bf16[640,256]{1,0:T(8,128)(2,1)} %q_hbm.1, bf16[640,256]{1,0:T(8,128)(2,1)} %k_hbm.1, bf16[640,256]{1,0:T(8,128)(2,1)} %v_hbm.1, ...), custom_call_target="tpu_custom_call" | custom-call | flops 20999999488 | bytes 14000000 | tf_op jit(solution)/shard_map/pallas_call | solution.py:656
  144.1 1.8 %copy.12 = bf16[320,640]{1,0:T(8,128)(2,1)} copy(bf16[320,640]{1,0:T(8,128)(2,1)} %shard_map.100) | data formatting | bytes 819200

commit v6 on v3

--- a/solution.py
+++ b/solution.py
@@ -38,7 +38,7 @@
 def kernel(
     frame_map, band, go_hbm, wo_hbm, q_hbm, k_hbm, v_hbm, wq_hbm, wk_hbm, wv_hbm, out_ref,
     go, wo, kall, qall, vall, dall, vown, logs, dots, p, pt, dist, dacc, att, gq,
-    tops, sums, row_dot, in1, in2,
+    tops, sums, row_dot, sbuf, gt, in1, in2,
     load_sem, zs, zr, ys, yr, s1, r1, s2, r2,
 ):
     g = lax.axis_index("tensor")
@@ -136,9 +136,12 @@
         tensor_copy(half, m + 2, j, 2, g).wait_recv()
         tensor_copy(half, m + 3, j, 3, g).wait_recv()
 
+    columns = (slice(0, 256), slice(256, 512), slice(512, 640))
+
     def add_row(index):
         cols = pl.ds(pl.multiple_of(ring(z, offsets[index]) * 1280, 1280), 1280)
-        dacc[...] += dot(wo[:, cols], go[cols, :])
+        for at in columns:
+            dacc[:, at] += dot(wo[:, cols], go[cols, at])
 
     sibling = y * 2 + 1 - core
 
@@ -239,18 +242,41 @@
     def factor(h, n):
         return jnp.sum(jnp.where(lane == n, sums[h], 0.0), axis=1, keepdims=True)
 
-    def masked(scores, first, second):
-        one = jnp.where(dist[...] <= first, scores[:, :F], masked_score)
-        two = jnp.where(dist[...] <= second, scores[:, F:], masked_score)
-        return jnp.concatenate([one, two], axis=1)
+    def tile(t):
+        return slice(t * 128, (t + 1) * 128)
+
+    def chunk_rows(n, c):
+        return pl.ds(pl.multiple_of(n * 2 * F + c * 256, 256), 256)
+
+    def over_chunks(left, ref, n, h, work):
+        ready = dot_nt(left, head(ref, chunk_rows(n, 0), h))
+        for c in range(5):
+            coming = dot_nt(left, head(ref, chunk_rows(n, c + 1), h)) if c < 4 else None
+            work(c, ready)
+            ready = coming
+
+    def keep(value, t, widths):
+        return jnp.where(dist[:, tile(t % 5)] <= widths[t // 5], value, masked_score)
 
     def softmax(n, h):
         widths = [band[my_frame, frame_map[2 * n + k]] for k in (0, 1)]
-        scores = masked(dot_nt(head(qall, mine, h), head(kall, pair_rows(n), h)), *widths)
-        top = jnp.max(scores, axis=1, keepdims=True) * POWER
-        shifted = jnp.exp2(scores * POWER - top)
-        total = jnp.sum(shifted, axis=1, keepdims=True)
-        p[h, n] = low(shifted)
+        best = [jnp.full((F, HD), masked_score, jnp.float32)]
+
+        def work(c, scores):
+            for k in (0, 1):
+                t = 2 * c + k
+                kept = keep(scores[:, tile(k)], t, widths)
+                sbuf[:, tile(t)] = kept
+                best[0] = jnp.maximum(best[0], kept)
+
+        over_chunks(head(qall, mine, h), kall, n, h, work)
+        top = jnp.max(best[0], axis=1, keepdims=True) * POWER
+        total = jnp.zeros((F, HD), jnp.float32)
+        for t in range(10):
+            shifted = jnp.exp2(sbuf[:, tile(t)] * POWER - top)
+            p[h, n, :, tile(t)] = low(shifted)
+            total = total + shifted
+        total = jnp.sum(total, axis=1, keepdims=True)
         tops[h] = jnp.where(lane == n, top, tops[h])
         sums[h] = jnp.where(lane == n, total, sums[h])
 
@@ -264,24 +290,45 @@
 
     def key_side(n, h):
         widths = [band[frame_map[2 * n + k], my_frame] for k in (0, 1)]
-        scores = dot_nt(head(kall, mine, h), head(qall, pair_rows(n), h))
-        power = masked(scores * POWER - stat_row(logs, n, h), *widths)
-        pt[h, n] = low(jnp.exp2(power))
+        log_row = stat_row(logs, n, h)
+
+        def work(c, scores):
+            for k in (0, 1):
+                t = 2 * c + k
+                power = keep(scores[:, tile(k)] * POWER - log_row[:, tile(t)], t, widths)
+                pt[h, n, :, tile(t)] = low(jnp.exp2(power))
+
+        over_chunks(head(kall, mine, h), qall, n, h, work)
 
     def attend(n, h):
         att[h] += factor(h, n) * dot(p[h, n], head(vall, pair_rows(n), h))
 
     def query_grad(n, h):
-        grad = dot_nt(head(dall, mine, h), head(vall, pair_rows(n), h))
-        grad = low(grad - jnp.concatenate([row_dot[h]] * 10, axis=1))
-        gq[h] += factor(h, n) * dot(p[h, n] * grad, head(kall, pair_rows(n), h))
+        own = row_dot[h]
+        total = [jnp.zeros((F, HD), jnp.float32)]
+
+        def work(c, grad):
+            grad = jnp.concatenate([low(grad[:, tile(k)] - own) for k in (0, 1)], axis=1)
+            weight = p[h, n, :, c * 256:(c + 1) * 256]
+            total[0] = total[0] + dot(weight * grad, head(kall, chunk_rows(n, c), h))
+
+        over_chunks(head(dall, mine, h), vall, n, h, work)
+        gq[h] += factor(h, n) * total[0]
 
     def key_grad(n, h):
-        grad_rows = head(dall, pair_rows(n), h)
-        weight = pt[h, n]
-        grad = low(dot_nt(head(vown, slice(None), h), grad_rows) - stat_row(dots, n, h))
-        gv[h] += dot(weight, grad_rows)
-        gk[h] += dot(weight * grad, head(qall, pair_rows(n), h))
+        own_row = stat_row(dots, n, h)
+        total = [jnp.zeros((F, HD), jnp.float32)] * 2
+
+        def work(c, grad):
+            at = slice(c * 256, (c + 1) * 256)
+            weight = pt[h, n, :, at]
+            total[1] = total[1] + dot(weight, head(dall, chunk_rows(n, c), h))
+            grad = weight * low(grad - own_row[:, at])
+            total[0] = total[0] + dot(grad, head(qall, chunk_rows(n, c), h))
+
+        over_chunks(head(vown, slice(None), h), dall, n, h, work)
+        gk[h] += total[0]
+        gv[h] += total[1]
 
     barrier = pltpu.get_barrier_semaphore()
     for half in (0, 1):
@@ -364,11 +411,9 @@
     loads = [load(0, wq_hbm, kall), load(1, wk_hbm, vall)]
     for item in loads:
         item.start()
-    gt = [p.at[0, n, 0:256, 0:F] for n in range(3)]
-
     def to_gt(n, ref, scale):
         for h in (0, 1):
-            gt[n][h * HD:(h + 1) * HD, :] = low((ref[h] * scale).T)
+            gt[n * 256 + h * HD:n * 256 + (h + 1) * HD, :] = low((ref[h] * scale).T)
 
     to_gt(0, gq, SCALE)
     by_arrival((grads, products), key_grad, {})
@@ -399,12 +444,13 @@
 
     def multiply(dz):
         def one(i, carry):
-            rows = pl.ds(pl.multiple_of(ring(z, dz) * 1280 + i * F, F), F)
-            total = dot(kall[rows, :], gt[0][...]) + dot(vall[rows, :], gt[1][...])
-            go[rows, :] = low(total + dot(qall[rows, :], gt[2][...]))
+            rows = pl.ds(pl.multiple_of(ring(z, dz) * 1280 + i * 320, 320), 320)
+            left = jnp.concatenate([kall[rows, :], vall[rows, :], qall[rows, :]], axis=1)
+            for at in columns:
+                go[rows, at] = low(dot(left, gt[:, at]))
             return carry
 
-        lax.fori_loop(0, 2, one, 0)
+        lax.fori_loop(0, 4, one, 0)
 
     def first(m, half, d, e, step):
         n = half * 12 + m
@@ -532,6 +578,8 @@
             pltpu.VMEM((F, F), jnp.int32),
             pltpu.VMEM((256, F), jnp.float32),
             heads, heads, heads, heads, heads,
+            pltpu.VMEM((F, 2 * F), jnp.float32),
+            pltpu.VMEM((768, F), jnp.bfloat16),
             pltpu.VMEM((24, 160, F), jnp.bfloat16),
             pltpu.VMEM((12, 80, F), jnp.bfloat16),
             sems((6,)), sems((40,)), sems((40,)), sems((8 * ARRAYS,)), sems((8 * ARRAYS,)),

time: 140 us -> 140 us (level)
  no operation moved by 1% of the time
where the time goes in v6:
time: 140 us
  Pallas kernels  138 us (99%)
  local copies, waits for them, and re-layouts  1.79 us (1%)
    pallas_call x1, Pallas kernels, per_device(): pl.pallas_call(kernel, out_shape=jax.ShapeDtypeStruct((320, F), jnp.bfloa...  138 us

profile of v6, /device:TPU:0, one launch (start us, length us, event | category | flops | bytes accessed | tf_op | source)
XLA Modules:
  0.0 139.9 jit_solution(16500173524352809378)
XLA Ops:
  0.0 138.1 %shard_map.100 = bf16[320,640]{1,0:T(8,128)(2,1)} custom-call(s32[8]{0:T(128)} %frame_map.1, s32[8,8]{1,0:T(8,128)} %band.1, bf16[320,640]{1,0:T(8,128)(2,1)} %bitcast.1, bf16[256,5120]{1,0:T(8,128)(2,1)} %wo_hbm.1, bf16[640,256]{1,0:T(8,128)(2,1)} %q_hbm.1, bf16[640,256]{1,0:T(8,128)(2,1)} %k_hbm.1, bf16[640,256]{1,0:T(8,128)(2,1)} %v_hbm.1, ...), custom_call_target="tpu_custom_call" | custom-call | flops 20999999488 | bytes 14000000 | tf_op jit(solution)/shard_map/pallas_call | solution.py:566
  138.1 1.8 %copy.12 = bf16[320,640]{1,0:T(8,128)(2,1)} copy(bf16[320,640]{1,0:T(8,128)(2,1)} %shard_map.100) | data formatting | bytes 819200

commit v7 on v4

--- a/solution.py
+++ b/solution.py
@@ -9,6 +9,7 @@
 F = 640
 SCALE = HD ** -0.5
 POWER = SCALE * 1.4426950408889634
+CHUNKS = ((0, 384), (384, 256))
 ARRAYS = 6
 MESH = pl.DeviceIdType.MESH
 NT = (((1,), (1,)), ((), ()))
@@ -37,9 +38,9 @@
 
 def kernel(
     frame_map, band, go_hbm, wo_hbm, q_hbm, k_hbm, v_hbm, wq_hbm, wk_hbm, wv_hbm, out_ref,
-    go, wo, kall, qall, vall, dall, vown, logs, dots, p, pt, dist, dacc, att, gq,
-    tops, sums, row_dot, in1, in2,
-    load_sem, zs, zr, ys, yr, s1, r1, s2, r2,
+    go, wo, kall, qall, vall, dall, logs, dots, p, pt, dist, dacc, att, gq,
+    tops, sums, row_dot, gt, wbuf, in1, in2,
+    load_sem, zs, zr, ys, yr, wsem, s1, r1, s2, r2,
 ):
     g = lax.axis_index("tensor")
     z, x = g // 4, g % 4
@@ -60,8 +61,7 @@
         load(1, k_hbm, kall.at[mine]),
         load(2, q_hbm, qall.at[mine]),
         load(3, v_hbm, vall.at[mine]),
-        load(4, v_hbm, vown),
-        load(5, wo_hbm, wo),
+        load(4, wo_hbm, wo),
     ]
     for item in loads:
         item.start()
@@ -231,8 +231,9 @@
         rows = pl.ds(pl.multiple_of(me * 16 + h * 8, 8), 8)
         ref[rows, :] = jnp.broadcast_to(column, (F, HD)).T[0:8, :]
 
-    def factor(h, s):
-        return jnp.sum(jnp.where(lane == s, sums[h], 0.0), axis=1, keepdims=True)
+    def factor(h, s, at=0, count=F):
+        own = sums[h, at:at + count, :]
+        return jnp.sum(jnp.where(lane[at:at + count] == s, own, 0.0), axis=1, keepdims=True)
 
     def softmax(s):
         width = band[my_frame, frame_map[s]]
@@ -267,20 +268,24 @@
         for h in (0, 1):
             att[h] += factor(h, s) * dot(p[h, s], head(vall, slot_rows(s), h))
 
-    def query_grad(s):
+    def query_grad(c, s):
+        at, count = CHUNKS[c]
+        rows, own = pl.ds(at, count), pl.ds(pl.multiple_of(me * F + at, 128), count)
         for h in (0, 1):
-            grad = dot_nt(head(dall, mine, h), head(vall, slot_rows(s), h))
-            grad = wide(p[h, s]) * ((grad - row_dot[h, :, 0:1]) * factor(h, s))
-            gq[h] += dot(low(grad), head(kall, slot_rows(s), h))
-
-    def key_grad(s):
+            grad = dot_nt(head(dall, own, h), head(vall, slot_rows(s), h))
+            grad = low(grad - jnp.concatenate([row_dot[h, rows, :]] * 5, axis=1))
+            product = dot(p[h, s, rows, :] * grad, head(kall, slot_rows(s), h))
+            gq[h, rows, :] += factor(h, s, at, count) * product
+
+    def key_grad(c, s):
+        at, count = CHUNKS[c]
+        rows, own = pl.ds(at, count), pl.ds(pl.multiple_of(me * F + at, 128), count)
         for h in (0, 1):
             grad_rows = head(dall, slot_rows(s), h)
-            weight = pt[h, s]
-            grad = dot_nt(head(vown, slice(None), h), grad_rows)
-            grad = wide(weight) * (grad - stat_row(dots, s, h))
-            gv[h] += dot(weight, grad_rows)
-            gk[h] += dot(low(grad), head(qall, slot_rows(s), h))
+            weight = pt[h, s, rows, :]
+            grad = low(dot_nt(head(vall, own, h), grad_rows) - stat_row(dots, s, h))
+            gv[h, rows, :] += dot(weight, grad_rows)
+            gk[h, rows, :] += dot(weight * grad, head(qall, slot_rows(s), h))
 
     barrier = pltpu.get_barrier_semaphore()
     for half in (0, 1):
@@ -347,37 +352,10 @@
     for ref in (gk, gv):
         ref[...] = jnp.zeros_like(ref)
 
-    def query_step(s, carry):
-        query_grad(s)
-
-        @pl.when(s == 5)
-        def _():
-            grads.near()
-            products.near()
-
-        return carry
-
-    lax.fori_loop(0, 8, query_step, 0)
-    keys.drain()
-    values.drain()
-    loads = [load(0, wq_hbm, kall), load(1, wk_hbm, vall)]
-    for item in loads:
-        item.start()
-    gt = [p.at[0, n, 0:256] for n in range(3)]
-
-    def to_gt(n, ref, scale):
+    def to_gt(n, ref, scale, c):
+        rows = pl.ds(*CHUNKS[c])
         for h in (0, 1):
-            gt[n][h * HD:(h + 1) * HD, :] = low((ref[h] * scale).T)
-
-    to_gt(0, gq, SCALE)
-    by_arrival((grads, products), key_grad, {})
-    queries.drain()
-    loads.append(load(2, wv_hbm, qall))
-    loads[2].start()
-    to_gt(1, gk, SCALE)
-    to_gt(2, gv, 1.0)
-    for item in loads:
-        item.wait()
+            gt[n * 256 + h * HD:n * 256 + (h + 1) * HD, rows] = low((ref[h, rows, :] * scale).T)
 
     def drain(half):
         def one(i, carry):
@@ -387,35 +365,29 @@
 
         lax.fori_loop(0, 5, one, 0)
 
-    both(drain)
-
     def target(half, d, e):
         return block(1 - half, d, e)
 
-    def part(half, d, e, skip=0, count=160):
+    def part(c, half, d, e, skip=0, count=160):
         start = target(half, d, e) * 320 + half * 160 + skip
-        return go.at[pl.ds(pl.multiple_of(start, 16), count)]
-
-    def multiply(dz):
-        def one(i, carry):
-            rows = pl.ds(pl.multiple_of(ring(z, dz) * 1280 + i * F, F), F)
-            total = dot(kall[rows, :], gt[0][...]) + dot(vall[rows, :], gt[1][...])
-            go[rows, :] = low(total + dot(qall[rows, :], gt[2][...]))
-            return carry
-
-        lax.fori_loop(0, 2, one, 0)
-
-    def first(m, half, d, e, step):
+        return go.at[pl.ds(pl.multiple_of(start, 16), count), pl.ds(*CHUNKS[c])]
+
+    def got(c, ref, n):
+        return wide(ref[n, :, pl.ds(*CHUNKS[c])])
+
+    def first(c, m, half, d, e, step):
         n = half * 12 + m
         return pltpu.make_async_remote_copy(
-            src_ref=part(half, d, e), dst_ref=in1.at[n], send_sem=s1.at[n], recv_sem=r1.at[n],
+            src_ref=part(c, half, d, e), dst_ref=in1.at[n, :, pl.ds(*CHUNKS[c])],
+            send_sem=s1.at[c * 24 + n], recv_sem=r1.at[c * 24 + n],
             device_id={"tensor": target(half, step, 0)}, device_id_type=MESH,
         )
 
-    def second(m, half, e, skip, step):
+    def second(c, m, half, e, skip, step):
         n = half * 6 + m
         return pltpu.make_async_remote_copy(
-            src_ref=part(half, 0, e, skip, 80), dst_ref=in2.at[n], send_sem=s2.at[n], recv_sem=r2.at[n],
+            src_ref=part(c, half, 0, e, skip, 80), dst_ref=in2.at[n, :, pl.ds(*CHUNKS[c])],
+            send_sem=s2.at[c * 12 + n], recv_sem=r2.at[c * 12 + n],
             device_id={"tensor": target(half, 0, step)}, device_id_type=MESH,
         )
 
@@ -423,87 +395,156 @@
     alone = ((4, 1, 1, 1), (5, 3, 2, -1), (6, 1, 0, 1), (7, 3, 3, -1))
     summed = ((8, 1, 2, 1), (9, 3, 1, -1), (10, 1, 3, 1), (11, 3, 0, -1))
 
-    def send(half, messages):
+    def send(c, half, messages):
         for m, d, e, step in messages:
-            first(m, half, d, e, step).start()
-
-    multiply(2)
-    send(0, far)
-    send(1, (far[0], alone[1]))
+            first(c, m, half, d, e, step).start()
+
+    def block_rows(j):
+        k = j // 2
+        dz = (k % 2) * (1 - k // 2) + (1 - k % 2) * (2 + k // 2)
+        return pl.ds(pl.multiple_of(ring(z, dz) * 1280 + (j % 2) * F, F), F)
+
+    def fetch(j):
+        return [
+            pltpu.make_async_copy(src.at[block_rows(j)], wbuf.at[j % 2, n], wsem.at[j % 2, n])
+            for n, src in enumerate((wq_hbm, wk_hbm, wv_hbm))
+        ]
+
+    def start_fetch(j):
+        for item in fetch(j):
+            item.start()
+
+    def multiply(c):
+        tokens = pl.ds(*CHUNKS[c])
+
+        def one(j, carry):
+            for item in fetch(j):
+                item.wait()
+
+            @pl.when(j < 7)
+            def _():
+                start_fetch(j + 1)
+
+            left = jnp.concatenate([wbuf[j % 2, n] for n in range(3)], axis=1)
+            go[block_rows(j), tokens] = low(dot(left, gt[:, tokens]))
+            events = {
+                1: ((0, far), (1, (far[0], alone[1]))),
+                3: ((1, (far[1], alone[0])), (0, (alone[0], alone[2]))),
+                5: ((1, (far[2], alone[3])), (0, (alone[1], alone[3]))),
+                7: ((1, (far[3], alone[2])),),
+            }
+            for when in events:
+                @pl.when(j == when)
+                def _(when=when):
+                    for half, messages in events[when]:
+                        send(c, half, messages)
+
+            return carry
+
+        lax.fori_loop(0, 8, one, 0)
+
+    def pass_on(c, message):
+        m, d, e, step = message
+
+        def one(half):
+            first(c, m - 8, half, d, e, step).wait_recv()
+            ref = part(c, half, d, e)
+            ref[...] = low(wide(ref[...]) + got(c, in1, half * 12 + m - 8))
+            first(c, m, half, d, e, step).start()
+
+        both(one)
+
+    def collect(c, half, e, up, down):
+        first(c, up, half, 0, e, 1).wait_recv()
+        first(c, down, half, 0, e, 1).wait_recv()
+        return wide(part(c, half, 0, e)[...]) + got(c, in1, half * 12 + up) + got(c, in1, half * 12 + down)
+
+    def collect_far(c, half):
+        part(c, half, 0, 2)[...] = low(collect(c, half, 2, 8, 5))
+        second(c, 0, half, 2, 0, 1).start()
+        second(c, 1, half, 2, 80, -1).start()
+
+    def collect_next(c, half):
+        total = collect(c, half, 1, 4, 9)
+        part(c, half, 0, 1)[...] = low(total)
+        second(c, 2, half, 1, 80, 1).start()
+        second(c, 0, half, 1, 0, 1).wait_recv()
+        part(c, half, 0, 1, 0, 80)[...] = low(total[0:80] + got(c, in2, half * 6))
+        second(c, 3, half, 1, 0, 1).start()
+
+    def collect_last(c, half):
+        total = collect(c, half, 3, 10, 7)
+        part(c, half, 0, 3)[...] = low(total)
+        second(c, 4, half, 3, 0, -1).start()
+        second(c, 1, half, 3, 80, -1).wait_recv()
+        part(c, half, 0, 3, 80, 80)[...] = low(total[80:160] + got(c, in2, half * 6 + 1))
+        second(c, 5, half, 3, 80, -1).start()
+
+    def collect_own(c, half):
+        total = collect(c, half, 0, 6, 11)
+        for m in (2, 3, 4, 5):
+            second(c, m, half, 0, 0, 1).wait_recv()
+        at = pl.multiple_of(half * 160, 16)
+        n, tokens = half * 6, pl.ds(*CHUNKS[c])
+        out_ref[pl.ds(at, 80), tokens] = low(total[0:80] + (got(c, in2, n + 3) + got(c, in2, n + 4)))
+        out_ref[pl.ds(at + 80, 80), tokens] = low(
+            total[80:160] + (got(c, in2, n + 2) + got(c, in2, n + 5))
+        )
+
+    def scatter_steps(c):
+        steps = [lambda message=message: pass_on(c, message) for message in summed]
+        for collector in (collect_far, collect_next, collect_last, collect_own):
+            steps.append(lambda collector=collector: both(lambda half: collector(c, half)))
+        return steps
+
+    def eight(body, events):
+        def one(s, carry):
+            body(s)
+            for when in events:
+                @pl.when(s == when)
+                def _(when=when):
+                    events[when]()
+
+            return carry
+
+        lax.fori_loop(0, 8, one, 0)
+
+    def grads_near():
+        grads.near()
+        products.near()
+
+    start_fetch(0)
+    eight(lambda s: query_grad(0, s), {6: grads_near})
+    to_gt(0, gq, SCALE, 0)
+    both(drain)
+    by_arrival((grads, products), lambda s: key_grad(0, s), {})
+    to_gt(1, gk, SCALE, 0)
+    to_gt(2, gv, 1.0, 0)
+    multiply(0)
+    start_fetch(0)
+    steps = scatter_steps(0)
+    eight(lambda s: query_grad(1, s), {3: steps[0], 4: steps[1], 5: steps[2], 6: steps[3]})
+    to_gt(0, gq, SCALE, 1)
+    eight(lambda s: key_grad(1, s), {1: steps[4], 3: steps[5], 5: steps[6], 7: steps[7]})
+    to_gt(1, gk, SCALE, 1)
+    to_gt(2, gv, 1.0, 1)
     multiply(1)
-    send(1, (far[1],))
-    send(0, (alone[0], alone[2]))
-    send(1, (alone[0], ))
-    multiply(3)
-    send(1, (far[2], alone[3]))
-    send(0, (alone[1], alone[3]))
-    multiply(0)
-    send(1, (far[3], alone[2]))
-
-    def pass_on(m, d, e, step):
-        def one(half):
-            first(m - 8, half, d, e, step).wait_recv()
-            ref = part(half, d, e)
-            ref[...] = low(wide(ref[...]) + wide(in1[half * 12 + m - 8]))
-            first(m, half, d, e, step).start()
-
-        both(one)
-
-    for message in summed:
-        pass_on(*message)
-
-    def collect(half, e, up, down):
-        first(up, half, 0, e, 1).wait_recv()
-        first(down, half, 0, e, 1).wait_recv()
-        return wide(part(half, 0, e)[...]) + wide(in1[half * 12 + up]) + wide(in1[half * 12 + down])
-
-    def collect_far(half):
-        total = collect(half, 2, 8, 5)
-        part(half, 0, 2)[...] = low(total)
-        second(0, half, 2, 0, 1).start()
-        second(1, half, 2, 80, -1).start()
-
-    def collect_next(half):
-        total = collect(half, 1, 4, 9)
-        part(half, 0, 1)[...] = low(total)
-        second(2, half, 1, 80, 1).start()
-        total_low = total[0:80]
-        second(0, half, 1, 0, 1).wait_recv()
-        part(half, 0, 1, 0, 80)[...] = low(total_low + wide(in2[half * 6]))
-        second(3, half, 1, 0, 1).start()
-
-    def collect_last(half):
-        total = collect(half, 3, 10, 7)
-        part(half, 0, 3)[...] = low(total)
-        second(4, half, 3, 0, -1).start()
-        total_high = total[80:160]
-        second(1, half, 3, 80, -1).wait_recv()
-        part(half, 0, 3, 80, 80)[...] = low(total_high + wide(in2[half * 6 + 1]))
-        second(5, half, 3, 80, -1).start()
-
-    def collect_own(half):
-        total = collect(half, 0, 6, 11)
-        for m in (2, 3, 4, 5):
-            second(m, half, 0, 0, 1).wait_recv()
-        at = pl.multiple_of(half * 160, 16)
-        n = half * 6
-        out_ref[pl.ds(at, 80), :] = low(total[0:80] + (wide(in2[n + 3]) + wide(in2[n + 4])))
-        out_ref[pl.ds(at + 80, 80), :] = low(total[80:160] + (wide(in2[n + 2]) + wide(in2[n + 5])))
-
-    for step in (collect_far, collect_next, collect_last, collect_own):
-        both(step)
+    for step in scatter_steps(1):
+        step()
 
     def sent1(m, carry):
-        first(m, 0, 0, 0, 1).wait_send()
+        for c in (0, 1):
+            first(c, m, 0, 0, 0, 1).wait_send()
         return carry
 
     def sent2(m, carry):
-        second(m, 0, 0, 0, 1).wait_send()
+        for c in (0, 1):
+            second(c, m, 0, 0, 0, 1).wait_send()
         return carry
 
     lax.fori_loop(0, 24, sent1, 0)
     lax.fori_loop(0, 12, sent2, 0)
-    for item in (grads, totals, products):
+    for item in (keys, queries, values, grads, totals, products):
         item.drain()
 
 
@@ -525,16 +566,17 @@
             pltpu.VMEM((5120, F), jnp.bfloat16),
             pltpu.VMEM((256, 5120), jnp.bfloat16),
             gathered, gathered, gathered, gathered,
-            pltpu.VMEM((F, 256), jnp.bfloat16),
             stats, stats,
             pairs, pairs,
             pltpu.VMEM((F, F), jnp.int32),
             pltpu.VMEM((256, F), jnp.float32),
             heads, heads, heads, heads, heads,
+            pltpu.VMEM((768, F), jnp.bfloat16),
+            pltpu.VMEM((2, 3, F, 256), jnp.bfloat16),
             pltpu.VMEM((24, 160, F), jnp.bfloat16),
             pltpu.VMEM((12, 80, F), jnp.bfloat16),
             sems((6,)), sems((40,)), sems((40,)), sems((8 * ARRAYS,)), sems((8 * ARRAYS,)),
-            sems((24,)), sems((24,)), sems((12,)), sems((12,)),
+            sems((2, 3)), sems((48,)), sems((48,)), sems((24,)), sems((24,)),
         ],
         compiler_params=pltpu.CompilerParams(
             collective_id=0, has_side_effects=True, vmem_limit_bytes=64 * 1024 * 1024

time: 137 us -> 142 us (1.036)
  Pallas kernels: 135 us -> 140 us
    pallas_call x1, Pallas kernels: 135 us -> 140 us  [per_device(): pl.pallas_call(kernel, out_shape=jax.ShapeDtypeStruct((320, F), jnp.bfloa...]
where the time goes in v7:
time: 142 us; the launch traced here: 141 us
  Pallas kernels  140 us (99%)
  local copies, waits for them, and re-layouts  1.79 us (1%)
    pallas_call x1, Pallas kernels, per_device(): pl.pallas_call(kernel, out_shape=jax.ShapeDtypeStruct((320, F), jnp.bfloa...  140 us

profile of v7, /device:TPU:0, one launch (start us, length us, event | category | flops | bytes accessed | tf_op | source)
XLA Modules:
  0.0 141.4 jit_solution(1867372429633324951)
XLA Ops:
  0.0 139.6 %shard_map.100 = bf16[320,640]{1,0:T(8,128)(2,1)} custom-call(s32[8]{0:T(128)} %frame_map.1, s32[8,8]{1,0:T(8,128)} %band.1, bf16[320,640]{1,0:T(8,128)(2,1)} %bitcast.1, bf16[256,5120]{1,0:T(8,128)(2,1)} %wo_hbm.1, bf16[640,256]{1,0:T(8,128)(2,1)} %q_hbm.1, bf16[640,256]{1,0:T(8,128)(2,1)} %k_hbm.1, bf16[640,256]{1,0:T(8,128)(2,1)} %v_hbm.1, ...), custom_call_target="tpu_custom_call" | custom-call | flops 20999999488 | bytes 14000000 | tf_op jit(solution)/shard_map/pallas_call | solution.py:560
  139.6 1.8 %copy.12 = bf16[320,640]{1,0:T(8,128)(2,1)} copy(bf16[320,640]{1,0:T(8,128)(2,1)} %shard_map.100) | data formatting | bytes 819200

commit v8 on v4

--- a/solution.py
+++ b/solution.py
@@ -45,6 +45,12 @@
     z, x = g // 4, g % 4
     me = lax.axis_index("tm")
     y, core = me // 2, me % 2
+    at_z = [z] + [ring(z, step) for step in (1, 2, 3)]
+    at_x = [x] + [ring(x, step) for step in (1, 2, 3)]
+    blocks = [[at_z[dz] * 4 + at_x[dx] for dx in range(4)] for dz in range(4)]
+    block_rows = [[blocks[dz][dx] * 320 for dx in range(4)] for dz in range(4)]
+    lines = [at_z[dz] * 1280 for dz in range(4)]
+    slots = [[ring(y, hop) * 2 + c for c in (core, 1 - core)] for hop in range(4)]
     my_frame = frame_map[me]
 
     def slot_rows(s):
@@ -67,25 +73,26 @@
         item.start()
 
     def block(half, d, e):
-        zz = ring(z, d * half + e * (1 - half))
-        xx = ring(x, d * (1 - half) + e * half)
-        return zz * 4 + xx
-
-    def tensor_copy(half, m, j, kind, target):
-        start = j * 320 + half * 160 + (80 if kind == 3 else 0)
+        dz, dx = (d, e) if half else (e, d)
+        return dz % 4, dx % 4
+
+    def device(at):
+        return (me, blocks[at[0]][at[1]])
+
+    def tensor_copy(half, m, at, kind, target):
+        start = block_rows[at[0]][at[1]] + (half * 160 + (80 if kind == 3 else 0))
         ref = go.at[pl.ds(pl.multiple_of(start, 16), 160 if kind < 2 else 80)]
         n = half * 20 + m
         return pltpu.make_async_remote_copy(
             src_ref=ref, dst_ref=ref, send_sem=zs.at[n], recv_sem=zr.at[n],
-            device_id={"tensor": target}, device_id_type=MESH,
+            device_id=device(target), device_id_type=MESH,
         )
 
     def both(step):
-        def one(half, carry):
+        for half in (0, 1):
             step(half)
-            return carry
-
-        lax.fori_loop(0, 2, one, 0)
+
+    here = (0, 0)
 
     def spread(half, index, d):
         j = block(half, d, 0)
@@ -94,26 +101,26 @@
         tensor_copy(half, m + 1, j, 1, block(half, 0, -1)).start()
 
     def tensor_start(half):
-        tensor_copy(half, 0, g, 0, block(half, 1, 0)).start()
-        tensor_copy(half, 1, g, 1, block(half, -1, 0)).start()
+        tensor_copy(half, 0, here, 0, block(half, 1, 0)).start()
+        tensor_copy(half, 1, here, 1, block(half, -1, 0)).start()
 
     def tensor_next(half):
         spread(half, 0, 0)
 
     def tensor_near(half):
         j = block(half, -1, 0)
-        tensor_copy(half, 0, j, 0, g).wait_recv()
+        tensor_copy(half, 0, j, 0, here).wait_recv()
         tensor_copy(half, 2, j, 2, block(half, 1, 0)).start()
         spread(half, 1, -1)
         j = block(half, 1, 0)
-        tensor_copy(half, 1, j, 1, g).wait_recv()
+        tensor_copy(half, 1, j, 1, here).wait_recv()
         tensor_copy(half, 3, j, 3, block(half, -1, 0)).start()
         spread(half, 2, 1)
 
     def tensor_far(half):
         j = block(half, 2, 0)
-        tensor_copy(half, 2, j, 2, g).wait_recv()
-        tensor_copy(half, 3, j, 3, g).wait_recv()
+        tensor_copy(half, 2, j, 2, here).wait_recv()
+        tensor_copy(half, 3, j, 3, here).wait_recv()
         spread(half, 3, 2)
 
     offsets = (0, -1, 1, 2)
@@ -122,10 +129,10 @@
         def step(half):
             m, d = 4 + 4 * index, offsets[index]
             j = block(half, d, -1)
-            tensor_copy(half, m, j, 0, g).wait_recv()
+            tensor_copy(half, m, j, 0, here).wait_recv()
             tensor_copy(half, m + 2, j, 2, block(half, 0, 1)).start()
             j = block(half, d, 1)
-            tensor_copy(half, m + 1, j, 1, g).wait_recv()
+            tensor_copy(half, m + 1, j, 1, here).wait_recv()
             tensor_copy(half, m + 3, j, 3, block(half, 0, -1)).start()
 
         both(step)
@@ -133,17 +140,17 @@
     def finish(half, index):
         m, d = 4 + 4 * index, offsets[index]
         j = block(half, d, 2)
-        tensor_copy(half, m + 2, j, 2, g).wait_recv()
-        tensor_copy(half, m + 3, j, 3, g).wait_recv()
+        tensor_copy(half, m + 2, j, 2, here).wait_recv()
+        tensor_copy(half, m + 3, j, 3, here).wait_recv()
 
     def add_row(index):
-        cols = pl.ds(pl.multiple_of(ring(z, offsets[index]) * 1280, 1280), 1280)
+        cols = pl.ds(pl.multiple_of(lines[offsets[index] % 4], 1280), 1280)
         dacc[...] += dot(wo[:, cols], go[cols, :])
 
-    sibling = y * 2 + 1 - core
+    sibling = slots[0][1]
 
     def at_y(step):
-        return ring(y, step) * 2 + core
+        return slots[step % 4][0]
 
     class Gather:
         def __init__(self, array, ref, rows):
@@ -158,7 +165,7 @@
             n = self.array * 8 + m
             return pltpu.make_async_remote_copy(
                 src_ref=ref, dst_ref=ref, send_sem=ys.at[n], recv_sem=yr.at[n],
-                device_id={"tm": target}, device_id_type=MESH,
+                device_id=(target, g), device_id_type=MESH,
             )
 
         def start(self):
@@ -181,8 +188,7 @@
 
         def from_sibling(self, *messages):
             for m in messages:
-                slot = ring(y, (0, -1, 1, 2)[m - 4]) * 2 + 1 - core
-                self.copy(m, slot, me).wait_recv()
+                self.copy(m, slots[(0, -1, 1, 2)[m - 4] % 4][1], me).wait_recv()
 
         def drain(self):
             for m in range(8):
@@ -194,10 +200,11 @@
 
     def by_arrival(gathers, body, events):
         def step(n, carry):
-            ring_at = (n + 2) // 4
-            hop = (ring_at % 2) * (2 * (n % 2) - 1) + (ring_at // 2) * 2
-            other = (1 - ring_at % 2) * (n % 2) + (ring_at % 2) * (((n + 2) // 2) % 2)
-            slot = ring(y, hop) * 2 + (core + other) % 2
+            ring_at = lax.div(n + 2, 4)
+            odd = lax.rem(n, 2)
+            hop = lax.rem(ring_at, 2) * (2 * odd - 1) + lax.div(ring_at, 2) * 2
+            other = (1 - lax.rem(ring_at, 2)) * odd + lax.rem(ring_at, 2) * lax.rem(lax.div(n + 2, 2), 2)
+            slot = ring(y, hop) * 2 + lax.rem(core + other, 2)
             waits = {
                 1: lambda item: item.from_sibling(4),
                 4: lambda item: item.from_sibling(5, 6),
@@ -286,10 +293,10 @@
     for half in (0, 1):
         for step in (1, -1):
             pl.semaphore_signal(
-                barrier, inc=1, device_id={"tensor": block(half, step, 0)}, device_id_type=MESH
+                barrier, inc=1, device_id=device(block(half, step, 0)), device_id_type=MESH
             )
     for target in (at_y(1), at_y(-1), sibling):
-        pl.semaphore_signal(barrier, inc=1, device_id={"tm": target}, device_id_type=MESH)
+        pl.semaphore_signal(barrier, inc=1, device_id=(target, g), device_id_type=MESH)
     loads[0].wait()
     loads[1].wait()
     pl.semaphore_wait(barrier, 7)
@@ -380,12 +387,9 @@
         item.wait()
 
     def drain(half):
-        def one(i, carry):
+        for i in range(5):
             for kind in range(4):
-                tensor_copy(half, 4 * i + kind, g, kind, g).wait_send()
-            return carry
-
-        lax.fori_loop(0, 5, one, 0)
+                tensor_copy(half, 4 * i + kind, here, kind, here).wait_send()
 
     both(drain)
 
@@ -393,12 +397,13 @@
         return block(1 - half, d, e)
 
     def part(half, d, e, skip=0, count=160):
-        start = target(half, d, e) * 320 + half * 160 + skip
+        dz, dx = target(half, d, e)
+        start = block_rows[dz][dx] + (half * 160 + skip)
         return go.at[pl.ds(pl.multiple_of(start, 16), count)]
 
     def multiply(dz):
         def one(i, carry):
-            rows = pl.ds(pl.multiple_of(ring(z, dz) * 1280 + i * F, F), F)
+            rows = pl.ds(pl.multiple_of(lines[dz] + i * F, F), F)
             total = dot(kall[rows, :], gt[0][...]) + dot(vall[rows, :], gt[1][...])
             go[rows, :] = low(total + dot(qall[rows, :], gt[2][...]))
             return carry
@@ -409,14 +414,14 @@
         n = half * 12 + m
         return pltpu.make_async_remote_copy(
             src_ref=part(half, d, e), dst_ref=in1.at[n], send_sem=s1.at[n], recv_sem=r1.at[n],
-            device_id={"tensor": target(half, step, 0)}, device_id_type=MESH,
+            device_id=device(target(half, step, 0)), device_id_type=MESH,
         )
 
     def second(m, half, e, skip, step):
         n = half * 6 + m
         return pltpu.make_async_remote_copy(
             src_ref=part(half, 0, e, skip, 80), dst_ref=in2.at[n], send_sem=s2.at[n], recv_sem=r2.at[n],
-            device_id={"tensor": target(half, 0, step)}, device_id_type=MESH,
+            device_id=device(target(half, 0, step)), device_id_type=MESH,
         )
 
     far = ((0, 2, 2, 1), (1, 2, 1, -1), (2, 2, 3, 1), (3, 2, 0, -1))
@@ -485,7 +490,7 @@
         total = collect(half, 0, 6, 11)
         for m in (2, 3, 4, 5):
             second(m, half, 0, 0, 1).wait_recv()
-        at = pl.multiple_of(half * 160, 16)
+        at = half * 160
         n = half * 6
         out_ref[pl.ds(at, 80), :] = low(total[0:80] + (wide(in2[n + 3]) + wide(in2[n + 4])))
         out_ref[pl.ds(at + 80, 80), :] = low(total[80:160] + (wide(in2[n + 2]) + wide(in2[n + 5])))
@@ -493,16 +498,11 @@
     for step in (collect_far, collect_next, collect_last, collect_own):
         both(step)
 
-    def sent1(m, carry):
-        first(m, 0, 0, 0, 1).wait_send()
-        return carry
-
-    def sent2(m, carry):
-        second(m, 0, 0, 0, 1).wait_send()
-        return carry
-
-    lax.fori_loop(0, 24, sent1, 0)
-    lax.fori_loop(0, 12, sent2, 0)
+    for half in (0, 1):
+        for m in range(12):
+            first(m, half, 0, 0, 1).wait_send()
+        for m in range(6):
+            second(m, half, 0, 0, 1).wait_send()
     for item in (grads, totals, products):
         item.drain()
 

time: 137 us -> 137 us (level)
  no operation moved by 1% of the time
where the time goes in v8:
time: 137 us
  Pallas kernels  135 us (99%)
  local copies, waits for them, and re-layouts  1.79 us (1%)
    pallas_call x1, Pallas kernels, per_device(): pl.pallas_call(kernel, out_shape=jax.ShapeDtypeStruct((320, F), jnp.bfloa...  135 us

profile of v8, /device:TPU:0, one launch (start us, length us, event | category | flops | bytes accessed | tf_op | source)
XLA Modules:
  0.0 136.6 jit_solution(13773015432753696786)
XLA Ops:
  0.0 134.8 %shard_map.100 = bf16[320,640]{1,0:T(8,128)(2,1)} custom-call(s32[8]{0:T(128)} %frame_map.1, s32[8,8]{1,0:T(8,128)} %band.1, bf16[320,640]{1,0:T(8,128)(2,1)} %bitcast.1, bf16[256,5120]{1,0:T(8,128)(2,1)} %wo_hbm.1, bf16[640,256]{1,0:T(8,128)(2,1)} %q_hbm.1, bf16[640,256]{1,0:T(8,128)(2,1)} %k_hbm.1, bf16[640,256]{1,0:T(8,128)(2,1)} %v_hbm.1, ...), custom_call_target="tpu_custom_call" | custom-call | flops 20999999488 | bytes 14000000 | tf_op jit(solution)/shard_map/pallas_call | solution.py:519
  134.8 1.8 %copy.12 = bf16[320,640]{1,0:T(8,128)(2,1)} copy(bf16[320,640]{1,0:T(8,128)(2,1)} %shard_map.100) | data formatting | bytes 819200

commit v9 on v7

--- a/solution.py
+++ b/solution.py
@@ -406,7 +406,7 @@
 
     def fetch(j):
         return [
-            pltpu.make_async_copy(src.at[block_rows(j)], wbuf.at[j % 2, n], wsem.at[j % 2, n])
+            pltpu.make_async_copy(src.at[block_rows(j)], wbuf.at[j % 3, n], wsem.at[j % 3, n])
             for n, src in enumerate((wq_hbm, wk_hbm, wv_hbm))
         ]
 
@@ -421,12 +421,13 @@
             for item in fetch(j):
                 item.wait()
 
-            @pl.when(j < 7)
+            left = jnp.concatenate([wbuf[j % 3, n] for n in range(3)], axis=1)
+            go[block_rows(j), tokens] = low(dot(left, gt[:, tokens]))
+
+            @pl.when(j < 5)
             def _():
-                start_fetch(j + 1)
-
-            left = jnp.concatenate([wbuf[j % 2, n] for n in range(3)], axis=1)
-            go[block_rows(j), tokens] = low(dot(left, gt[:, tokens]))
+                start_fetch(j + 3)
+
             events = {
                 1: ((0, far), (1, (far[0], alone[1]))),
                 3: ((1, (far[1], alone[0])), (0, (alone[0], alone[2]))),
@@ -513,7 +514,8 @@
         grads.near()
         products.near()
 
-    start_fetch(0)
+    for j in range(3):
+        start_fetch(j)
     eight(lambda s: query_grad(0, s), {6: grads_near})
     to_gt(0, gq, SCALE, 0)
     both(drain)
@@ -521,15 +523,16 @@
     to_gt(1, gk, SCALE, 0)
     to_gt(2, gv, 1.0, 0)
     multiply(0)
-    start_fetch(0)
+    for j in range(3):
+        start_fetch(j)
     steps = scatter_steps(0)
-    eight(lambda s: query_grad(1, s), {3: steps[0], 4: steps[1], 5: steps[2], 6: steps[3]})
+    eight(lambda s: query_grad(1, s), {4: steps[0], 5: steps[1], 6: steps[2], 7: steps[3]})
     to_gt(0, gq, SCALE, 1)
-    eight(lambda s: key_grad(1, s), {1: steps[4], 3: steps[5], 5: steps[6], 7: steps[7]})
+    eight(lambda s: key_grad(1, s), {6: steps[4]})
     to_gt(1, gk, SCALE, 1)
     to_gt(2, gv, 1.0, 1)
     multiply(1)
-    for step in scatter_steps(1):
+    for step in steps[5:] + scatter_steps(1):
         step()
 
     def sent1(m, carry):
@@ -572,11 +575,11 @@
             pltpu.VMEM((256, F), jnp.float32),
             heads, heads, heads, heads, heads,
             pltpu.VMEM((768, F), jnp.bfloat16),
-            pltpu.VMEM((2, 3, F, 256), jnp.bfloat16),
+            pltpu.VMEM((3, 3, F, 256), jnp.bfloat16),
             pltpu.VMEM((24, 160, F), jnp.bfloat16),
             pltpu.VMEM((12, 80, F), jnp.bfloat16),
             sems((6,)), sems((40,)), sems((40,)), sems((8 * ARRAYS,)), sems((8 * ARRAYS,)),
-            sems((2, 3)), sems((48,)), sems((48,)), sems((24,)), sems((24,)),
+            sems((3, 3)), sems((48,)), sems((48,)), sems((24,)), sems((24,)),
         ],
         compiler_params=pltpu.CompilerParams(
             collective_id=0, has_side_effects=True, vmem_limit_bytes=64 * 1024 * 1024

time: 142 us -> 137 us (0.965)
  Pallas kernels: 140 us -> 134 us
    pallas_call x1, Pallas kernels: 140 us -> 134 us  [per_device(): pl.pallas_call(kernel, out_shape=jax.ShapeDtypeStruct((320, F), jnp.bfloa...]
where the time goes in v9:
time: 137 us; the launch traced here: 135 us
  Pallas kernels  134 us (98%)
  local copies, waits for them, and re-layouts  1.79 us (1%)
    pallas_call x1, Pallas kernels, per_device(): pl.pallas_call(kernel, out_shape=jax.ShapeDtypeStruct((320, F), jnp.bfloa...  134 us

profile of v9, /device:TPU:0, one launch (start us, length us, event | category | flops | bytes accessed | tf_op | source)
XLA Modules:
  0.0 135.3 jit_solution(16616874913248743380)
XLA Ops:
  0.0 133.5 %shard_map.100 = bf16[320,640]{1,0:T(8,128)(2,1)} custom-call(s32[8]{0:T(128)} %frame_map.1, s32[8,8]{1,0:T(8,128)} %band.1, bf16[320,640]{1,0:T(8,128)(2,1)} %bitcast.1, bf16[256,5120]{1,0:T(8,128)(2,1)} %wo_hbm.1, bf16[640,256]{1,0:T(8,128)(2,1)} %q_hbm.1, bf16[640,256]{1,0:T(8,128)(2,1)} %k_hbm.1, bf16[640,256]{1,0:T(8,128)(2,1)} %v_hbm.1, ...), custom_call_target="tpu_custom_call" | custom-call | flops 20999999488 | bytes 14000000 | tf_op jit(solution)/shard_map/pallas_call | solution.py:563
  133.5 1.8 %copy.12 = bf16[320,640]{1,0:T(8,128)(2,1)} copy(bf16[320,640]{1,0:T(8,128)(2,1)} %shard_map.100) | data formatting | bytes 819200

commit v10 on v9

--- a/solution.py
+++ b/solution.py
@@ -320,22 +320,15 @@
     )
     combine()
     totals.start()
-
-    def queries_near():
-        queries.near()
-        values.start()
-        totals.near()
-
+    queries.near()
+    values.start()
+    totals.near()
     by_arrival(
         (queries, totals), key_side,
-        {2: queries_near, 4: lambda: forward(1), 7: lambda: forward(2)},
+        {3: lambda: forward(1), 5: lambda: forward(2), 7: lambda: forward(3)},
     )
-    forward(3)
-
-    def values_near():
-        values.near()
-
-    by_arrival((values,), attend, {2: values_near})
+    values.near()
+    by_arrival((values,), attend, {})
     for index in range(4):
         finish(0, index)
     for index in range(4):
@@ -516,7 +509,7 @@
 
     for j in range(3):
         start_fetch(j)
-    eight(lambda s: query_grad(0, s), {6: grads_near})
+    eight(lambda s: query_grad(0, s), {7: grads_near})
     to_gt(0, gq, SCALE, 0)
     both(drain)
     by_arrival((grads, products), lambda s: key_grad(0, s), {})

time: 137 us -> 133 us (0.971)
  Pallas kernels: 134 us -> 130 us
    pallas_call x1, Pallas kernels: 134 us -> 130 us  [per_device(): pl.pallas_call(kernel, out_shape=jax.ShapeDtypeStruct((320, F), jnp.bfloa...]
where the time goes in v10:
time: 133 us; the launch traced here: 132 us
  Pallas kernels  130 us (98%)
  local copies, waits for them, and re-layouts  1.79 us (1%)
    pallas_call x1, Pallas kernels, per_device(): pl.pallas_call(kernel, out_shape=jax.ShapeDtypeStruct((320, F), jnp.bfloa...  130 us

profile of v10, /device:TPU:0, one launch (start us, length us, event | category | flops | bytes accessed | tf_op | source)
XLA Modules:
  0.0 132.0 jit_solution(12711045639659353487)
XLA Ops:
  0.0 130.2 %shard_map.100 = bf16[320,640]{1,0:T(8,128)(2,1)} custom-call(s32[8]{0:T(128)} %frame_map.1, s32[8,8]{1,0:T(8,128)} %band.1, bf16[320,640]{1,0:T(8,128)(2,1)} %bitcast.1, bf16[256,5120]{1,0:T(8,128)(2,1)} %wo_hbm.1, bf16[640,256]{1,0:T(8,128)(2,1)} %q_hbm.1, bf16[640,256]{1,0:T(8,128)(2,1)} %k_hbm.1, bf16[640,256]{1,0:T(8,128)(2,1)} %v_hbm.1, ...), custom_call_target="tpu_custom_call" | custom-call | flops 20999999488 | bytes 14000000 | tf_op jit(solution)/shard_map/pallas_call | solution.py:556
  130.2 1.8 %copy.12 = bf16[320,640]{1,0:T(8,128)(2,1)} copy(bf16[320,640]{1,0:T(8,128)(2,1)} %shard_map.100) | data formatting | bytes 819200

commit v11 on v10

--- a/solution.py
+++ b/solution.py
@@ -318,22 +318,26 @@
         (keys,), softmax,
         {2: keys_near, 5: lambda: both(tensor_far), 7: lambda: forward(0)},
     )
+    queries.near()
+    values.start()
     combine()
     totals.start()
-    queries.near()
-    values.start()
     totals.near()
     by_arrival(
         (queries, totals), key_side,
         {3: lambda: forward(1), 5: lambda: forward(2), 7: lambda: forward(3)},
     )
     values.near()
-    by_arrival((values,), attend, {})
+
+    def near_row(index):
+        finish(1, index)
+        add_row(index)
+
+    near_row(0)
+    by_arrival((values,), attend, {4: lambda: near_row(1), 6: lambda: near_row(2)})
     for index in range(4):
         finish(0, index)
-    for index in range(4):
-        finish(1, index)
-        add_row(index)
+    near_row(3)
     dall[mine, :] = low(dacc[...].T)
     grads.start()
     for h in (0, 1):
@@ -459,19 +463,23 @@
         second(c, 1, half, 2, 80, -1).start()
 
     def collect_next(c, half):
-        total = collect(c, half, 1, 4, 9)
-        part(c, half, 0, 1)[...] = low(total)
+        part(c, half, 0, 1)[...] = low(collect(c, half, 1, 4, 9))
         second(c, 2, half, 1, 80, 1).start()
+
+    def collect_last(c, half):
+        part(c, half, 0, 3)[...] = low(collect(c, half, 3, 10, 7))
+        second(c, 4, half, 3, 0, -1).start()
+
+    def add_next(c, half):
         second(c, 0, half, 1, 0, 1).wait_recv()
-        part(c, half, 0, 1, 0, 80)[...] = low(total[0:80] + got(c, in2, half * 6))
+        ref = part(c, half, 0, 1, 0, 80)
+        ref[...] = low(wide(ref[...]) + got(c, in2, half * 6))
         second(c, 3, half, 1, 0, 1).start()
 
-    def collect_last(c, half):
-        total = collect(c, half, 3, 10, 7)
-        part(c, half, 0, 3)[...] = low(total)
-        second(c, 4, half, 3, 0, -1).start()
+    def add_last(c, half):
         second(c, 1, half, 3, 80, -1).wait_recv()
-        part(c, half, 0, 3, 80, 80)[...] = low(total[80:160] + got(c, in2, half * 6 + 1))
+        ref = part(c, half, 0, 3, 80, 80)
+        ref[...] = low(wide(ref[...]) + got(c, in2, half * 6 + 1))
         second(c, 5, half, 3, 80, -1).start()
 
     def collect_own(c, half):
@@ -487,7 +495,7 @@
 
     def scatter_steps(c):
         steps = [lambda message=message: pass_on(c, message) for message in summed]
-        for collector in (collect_far, collect_next, collect_last, collect_own):
+        for collector in (collect_far, collect_next, collect_last, add_next, add_last, collect_own):
             steps.append(lambda collector=collector: both(lambda half: collector(c, half)))
         return steps
 
@@ -525,7 +533,8 @@
     to_gt(1, gk, SCALE, 1)
     to_gt(2, gv, 1.0, 1)
     multiply(1)
-    for step in steps[5:] + scatter_steps(1):
+    rest = scatter_steps(1)
+    for step in steps[5:9] + rest[:4] + steps[9:] + rest[4:]:
         step()
 
     def sent1(m, carry):

time: 133 us -> 133 us (level)
  no operation moved by 1% of the time
where the time goes in v11:
time: 133 us
  Pallas kernels  131 us (98%)
  local copies, waits for them, and re-layouts  1.79 us (1%)
    pallas_call x1, Pallas kernels, per_device(): pl.pallas_call(kernel, out_shape=jax.ShapeDtypeStruct((320, F), jnp.bfloa...  131 us

profile of v11, /device:TPU:0, one launch (start us, length us, event | category | flops | bytes accessed | tf_op | source)
XLA Modules:
  0.0 133.0 jit_solution(10893515089298680473)
XLA Ops:
  0.0 131.2 %shard_map.100 = bf16[320,640]{1,0:T(8,128)(2,1)} custom-call(s32[8]{0:T(128)} %frame_map.1, s32[8,8]{1,0:T(8,128)} %band.1, bf16[320,640]{1,0:T(8,128)(2,1)} %bitcast.1, bf16[256,5120]{1,0:T(8,128)(2,1)} %wo_hbm.1, bf16[640,256]{1,0:T(8,128)(2,1)} %q_hbm.1, bf16[640,256]{1,0:T(8,128)(2,1)} %k_hbm.1, bf16[640,256]{1,0:T(8,128)(2,1)} %v_hbm.1, ...), custom_call_target="tpu_custom_call" | custom-call | flops 20999999488 | bytes 14000000 | tf_op jit(solution)/shard_map/pallas_call | solution.py:565
  131.2 1.8 %copy.12 = bf16[320,640]{1,0:T(8,128)(2,1)} copy(bf16[320,640]{1,0:T(8,128)(2,1)} %shard_map.100) | data formatting | bytes 819200

commit v12 on v11

--- a/solution.py
+++ b/solution.py
@@ -9,7 +9,7 @@
 F = 640
 SCALE = HD ** -0.5
 POWER = SCALE * 1.4426950408889634
-CHUNKS = ((0, 384), (384, 256))
+CHUNKS = ((0, 256), (256, 384))
 ARRAYS = 6
 MESH = pl.DeviceIdType.MESH
 NT = (((1,), (1,)), ((), ()))

time: 133 us -> 136 us (1.023)
  Pallas kernels: 131 us -> 134 us
    pallas_call x1, Pallas kernels: 131 us -> 134 us  [per_device(): pl.pallas_call(kernel, out_shape=jax.ShapeDtypeStruct((320, F), jnp.bfloa...]
where the time goes in v12:
time: 136 us; the launch traced here: 135 us
  Pallas kernels  134 us (99%)
  local copies, waits for them, and re-layouts  1.79 us (1%)
    pallas_call x1, Pallas kernels, per_device(): pl.pallas_call(kernel, out_shape=jax.ShapeDtypeStruct((320, F), jnp.bfloa...  134 us

profile of v12, /device:TPU:0, one launch (start us, length us, event | category | flops | bytes accessed | tf_op | source)
XLA Modules:
  0.0 135.4 jit_solution(4218593278844969433)
XLA Ops:
  0.0 133.6 %shard_map.100 = bf16[320,640]{1,0:T(8,128)(2,1)} custom-call(s32[8]{0:T(128)} %frame_map.1, s32[8,8]{1,0:T(8,128)} %band.1, bf16[320,640]{1,0:T(8,128)(2,1)} %bitcast.1, bf16[256,5120]{1,0:T(8,128)(2,1)} %wo_hbm.1, bf16[640,256]{1,0:T(8,128)(2,1)} %q_hbm.1, bf16[640,256]{1,0:T(8,128)(2,1)} %k_hbm.1, bf16[640,256]{1,0:T(8,128)(2,1)} %v_hbm.1, ...), custom_call_target="tpu_custom_call" | custom-call | flops 20999999488 | bytes 14000000 | tf_op jit(solution)/shard_map/pallas_call | solution.py:565
  133.6 1.8 %copy.12 = bf16[320,640]{1,0:T(8,128)(2,1)} copy(bf16[320,640]{1,0:T(8,128)(2,1)} %shard_map.100) | data formatting | bytes 819200

commit v13 on v12

--- a/solution.py
+++ b/solution.py
@@ -9,7 +9,7 @@
 F = 640
 SCALE = HD ** -0.5
 POWER = SCALE * 1.4426950408889634
-CHUNKS = ((0, 256), (256, 384))
+CHUNKS = ((0, 512), (512, 128))
 ARRAYS = 6
 MESH = pl.DeviceIdType.MESH
 NT = (((1,), (1,)), ((), ()))

time: 136 us -> 134 us (0.985)
  Pallas kernels: 134 us -> 132 us
    pallas_call x1, Pallas kernels: 134 us -> 132 us  [per_device(): pl.pallas_call(kernel, out_shape=jax.ShapeDtypeStruct((320, F), jnp.bfloa...]
where the time goes in v13:
time: 134 us
  Pallas kernels  132 us (99%)
  local copies, waits for them, and re-layouts  1.79 us (1%)
    pallas_call x1, Pallas kernels, per_device(): pl.pallas_call(kernel, out_shape=jax.ShapeDtypeStruct((320, F), jnp.bfloa...  132 us

profile of v13, /device:TPU:0, one launch (start us, length us, event | category | flops | bytes accessed | tf_op | source)
XLA Modules:
  0.0 133.8 jit_solution(3769865317336032941)
XLA Ops:
  0.0 132.0 %shard_map.100 = bf16[320,640]{1,0:T(8,128)(2,1)} custom-call(s32[8]{0:T(128)} %frame_map.1, s32[8,8]{1,0:T(8,128)} %band.1, bf16[320,640]{1,0:T(8,128)(2,1)} %bitcast.1, bf16[256,5120]{1,0:T(8,128)(2,1)} %wo_hbm.1, bf16[640,256]{1,0:T(8,128)(2,1)} %q_hbm.1, bf16[640,256]{1,0:T(8,128)(2,1)} %k_hbm.1, bf16[640,256]{1,0:T(8,128)(2,1)} %v_hbm.1, ...), custom_call_target="tpu_custom_call" | custom-call | flops 20999999488 | bytes 14000000 | tf_op jit(solution)/shard_map/pallas_call | solution.py:565
  132.0 1.8 %copy.12 = bf16[320,640]{1,0:T(8,128)(2,1)} copy(bf16[320,640]{1,0:T(8,128)(2,1)} %shard_map.100) | data formatting | bytes 819200
